TPU v7x, 256 devices: a whole 4x4x8 slice. The times are simulated.
256 devices in a mesh: frame: 16 (over x, y), expert: 16 (over z, core).
Axes of the slice: x: 4, y: 4, z: 8, core: 2. Of those that a mesh axis runs over, the one named last changes fastest.
Arguments:
- upstream: bfloat16 [16, 2048, 2048], P('frame', 'expert'), may hold values from -6 to 6
- saved: bfloat16 [16, 2048, 2048], P('frame', 'expert'), may hold values from -6 to 6
- expert_ids: int32 [16, 2048, 2], P('frame', 'expert'), may hold values from 0 to 15, all different within a row; in each aligned block of 128 rows (0 to 127, 128 to 255, ..., all dimensions but the last counted through in order) at most 32 rows name the same one
- gates: float32 [16, 2048, 2], P('frame', 'expert'), may hold values from 0.1 to 0.9
- weight_in: bfloat16 [16, 2048, 1024], P('expert'), may hold values from -0.125 to 0.125
- weight_out: bfloat16 [16, 2048, 1024], P('expert'), may hold values from -0.1875 to 0.1875
- spatial_rate: bfloat16 [16, 2048, 2048], P('frame', 'expert'), may hold values from 0 to 1
- temporal_rate: float32 [16, 2048], replicated, may hold values from 0 to 4.5
- scan_order: int32 [2048], P('expert'), may hold values from 0 to 2047, as said below
Outputs:
- result: bfloat16 [16, 2048, 2048], P('frame', 'expert')
- grad_in: bfloat16 [16, 2048, 1024], P('expert', 'frame')
- grad_out: bfloat16 [16, 2048, 1024], P('expert', 'frame')
Inputs may be any that keep to these rules, and one draw needn't show every extreme that they name: `expert_ids`: each row names 2 different experts. Among the 128 rows of one device, no expert is named by more than 32 rows, and in some devices one expert is named by exactly 32. `scan_order`: each aligned block of 128 scan steps visits exactly the tokens of the same block, in some order.
All inputs are finite; a program needn't handle non-finite values.
Results may differ from a plain program's by a relative error of at most 0.006.
Values may be sent and summed in bfloat16 or wider, within the bound.
No kernel may reach another device: no remote copies, remote signals or barrier semaphores. Data moves between devices by JAX's collectives and lax.ppermute only.
A program may use at most 192 MiB of HBM per device.

v0:
```python
import functools
import math

import jax
import jax.numpy as jnp
from jax import lax
from jax.experimental import pallas as pl
from jax.experimental.pallas import tpu as pltpu
from jax.sharding import PartitionSpec as P

TOPK = 2
LANES = 128
SUB = 8
VMEM_LIMIT = 48 * 1024 * 1024

GELU_SCALE = 0.7978845608028654
GELU_CUBIC = 0.044715


def gelu_parts(pre):
    inner = GELU_SCALE * (pre + GELU_CUBIC * pre * pre * pre)
    tangent = jnp.tanh(inner)
    value = 0.5 * pre * (1.0 + tangent)
    slope = 0.5 * (1.0 + tangent) + 0.5 * pre * (1.0 - tangent * tangent) * GELU_SCALE * (
        1.0 + 3.0 * GELU_CUBIC * pre * pre
    )
    return (value, slope)


def column_product(left, right):
    return lax.dot_general(
        left, right, (((0,), (0,)), ((), ())), preferred_element_type=jnp.float32
    )


def iota(shape, dim):
    return lax.broadcasted_iota(jnp.int32, shape, dim)


def call(kernel, out_shape, name, **kw):
    return pl.pallas_call(
        kernel,
        out_shape=out_shape,
        name=name,
        compiler_params=pltpu.CompilerParams(vmem_limit_bytes=VMEM_LIMIT),
        **kw,
    )


def info_kernel(ids_col, rate, info, head):
    experts = info.shape[0]
    rows, width = rate.shape
    blocks = width // LANES
    slots = experts * 32
    expert_of = iota((rows, slots), 1) // 32
    slot_of = iota((rows, slots), 1) % 32
    token = iota((rows, slots), 0)
    hit = (ids_col[:, 0:1] == expert_of) | (ids_col[:, 1:2] == expert_of)
    before = (iota((rows, rows), 1) < iota((rows, rows), 0)).astype(jnp.bfloat16)
    rank = jnp.dot(
        before, hit.astype(jnp.float32).astype(jnp.bfloat16), preferred_element_type=jnp.float32
    )
    chosen = hit & (rank.astype(jnp.int32) == slot_of)
    row_of = (
        jnp.sum(jnp.where(chosen, (token + 1).astype(jnp.float32), 0.0), axis=0, keepdims=True) - 1.0
    )
    total = jnp.exp(-jnp.sum(rate[...].astype(jnp.float32), axis=0, keepdims=True))
    for b in range(blocks):
        head[b : b + 1, :] = total[:, b * LANES : (b + 1) * LANES]
    spread = head[...]
    for e in range(experts):
        info[e, 0:blocks, :] = spread
        info[e, blocks : blocks + 8, :] = jnp.zeros((8, LANES), jnp.float32)
        info[e, blocks : blocks + 1, 0:32] = row_of[:, e * 32 : (e + 1) * 32]


def send_kernel(ids_row, gates_row, upstream, send):
    slots = send.shape[0]
    rows, width = upstream.shape
    expert_of = iota((slots, rows), 0) // 32
    slot_of = iota((slots, rows), 0) % 32
    first = ids_row[0:1, :] == expert_of
    hit = first | (ids_row[1:2, :] == expert_of)
    before = (iota((rows, rows), 0) < iota((rows, rows), 1)).astype(jnp.bfloat16)
    rank = jnp.dot(
        hit.astype(jnp.float32).astype(jnp.bfloat16), before, preferred_element_type=jnp.float32
    )
    chosen = hit & (rank.astype(jnp.int32) == slot_of)
    gate = jnp.sum(
        jnp.where(chosen, jnp.where(first, gates_row[0:1, :], gates_row[1:2, :]), 0.0),
        axis=1,
        keepdims=True,
    )
    pick = chosen.astype(jnp.float32).astype(jnp.bfloat16)
    step = 512
    for c in range(0, width, step):
        part = jnp.dot(pick, upstream[:, c : c + step], preferred_element_type=jnp.float32)
        send[:, c : c + step] = (gate * part).astype(jnp.bfloat16)


def order_kernel(ids_col, order_col, upstream, undo, ordered):
    rows, slots = undo.shape
    expert_of = iota((rows, slots), 1) // 32
    slot_of = iota((rows, slots), 1) % 32
    hit = (ids_col[:, 0:1] == expert_of) | (ids_col[:, 1:2] == expert_of)
    before = (iota((rows, rows), 1) < iota((rows, rows), 0)).astype(jnp.bfloat16)
    rank = jnp.dot(
        before, hit.astype(jnp.float32).astype(jnp.bfloat16), preferred_element_type=jnp.float32
    )
    chosen = (hit & (rank.astype(jnp.int32) == slot_of)).astype(jnp.float32).astype(jnp.bfloat16)
    visit = (order_col[...] == iota((rows, rows), 1)).astype(jnp.float32).astype(jnp.bfloat16)
    undo[...] = jnp.dot(visit, chosen, preferred_element_type=jnp.float32).astype(jnp.bfloat16)
    ordered[...] = jnp.dot(visit, upstream[...], preferred_element_type=jnp.float32).astype(
        jnp.bfloat16
    )


def decay_kernel(rate, c1, c2, c4, cross, through):
    rows, width = rate.shape
    tiles = rows // SUB
    row = iota((SUB, LANES), 0)

    def column(b, _):
        at = pl.ds(pl.multiple_of(b * LANES, LANES), LANES)
        wide = rate[:, at].astype(jnp.float32)
        later = jnp.zeros((1, LANES), jnp.float32)
        beyond = jnp.zeros((SUB, LANES), jnp.float32)
        for tile in reversed(range(tiles)):
            here = pl.ds(tile * SUB, SUB)
            shifted = pltpu.roll(wide[tile * SUB : (tile + 1) * SUB], SUB - 1, 0)
            e1 = jnp.where(row < 7, shifted, beyond)
            beyond = shifted
            e2 = e1 + pltpu.roll(e1, SUB - 1, 0)
            e4 = e2 + pltpu.roll(e2, SUB - 2, 0)
            s1 = e1 + jnp.where(row < 7, pltpu.roll(e1, SUB - 1, 0), 0.0)
            s2 = s1 + jnp.where(row < 6, pltpu.roll(s1, SUB - 2, 0), 0.0)
            s4 = s2 + jnp.where(row < 4, pltpu.roll(s2, SUB - 4, 0), 0.0)
            c1[here, at] = jnp.where(row < 7, jnp.exp(-e1), 0.0)
            c2[here, at] = jnp.where(row < 6, jnp.exp(-e2), 0.0)
            c4[here, at] = jnp.where(row < 4, jnp.exp(-e4), 0.0)
            cross[here, at] = jnp.exp(-s4)
            through[here, at] = jnp.exp(-(s4 + later))
            later = later + s4[0:1]
        return 0

    lax.fori_loop(0, width // LANES, column, 0)


def gather_kernel(info, saved, picked):
    rows = saved.shape[0]
    row_of = info[0, 16:17, 0:32]
    pick = (iota((rows, 32), 0).astype(jnp.float32) == row_of).astype(jnp.float32)
    picked[...] = lax.dot_general(
        pick.astype(jnp.bfloat16),
        saved[...],
        (((0,), (0,)), ((), ())),
        preferred_element_type=jnp.float32,
    ).astype(jnp.bfloat16)


def undo_kernel(undo, returned, mixed):
    blocks = mixed.shape[0]
    pick = undo[...]
    step = 512
    for c in range(0, blocks * LANES, step):
        part = jnp.dot(pick, returned[:, c : c + step], preferred_element_type=jnp.float32).astype(
            jnp.bfloat16
        )
        for b in range(step // LANES):
            mixed[c // LANES + b] = part[:, b * LANES : (b + 1) * LANES]


def temporal_kernel(pencil, keep, inject, out):
    frames = pencil.shape[0]
    carry = jnp.zeros(pencil.shape[1:], jnp.float32)
    for f in reversed(range(frames)):
        total = pencil[f].astype(jnp.float32) + carry
        out[f] = (inject[f : f + 1, :] * total).astype(jnp.bfloat16)
        carry = keep[f : f + 1, :] * total


def scan_kernel(spatial, first_keep, weight, c1, c2, c4, cross, local, send, head):
    blocks, rows, _ = spatial.shape
    tiles = rows // SUB
    beyond = jnp.zeros((1, blocks * LANES), jnp.float32)
    for pair in reversed(range(tiles // 2)):
        wide = jnp.concatenate(
            [spatial[b, pair * 16 : pair * 16 + 16, :].astype(jnp.float32) for b in range(blocks)],
            axis=1,
        )
        for half in (1, 0):
            here = pl.ds(pair * 16 + half * SUB, SUB)
            value = wide[half * SUB : (half + 1) * SUB]
            value = value + c1[here, :] * pltpu.roll(value, SUB - 1, 0)
            value = value + c2[here, :] * pltpu.roll(value, SUB - 2, 0)
            value = value + c4[here, :] * pltpu.roll(value, SUB - 4, 0)
            value = value + cross[here, :] * beyond
            local[here, :] = value
            beyond = value[0:1]
    top = jnp.exp(-first_keep[0:1, :].astype(jnp.float32)) * beyond
    for b in range(blocks):
        head[b : b + 1, :] = top[:, b * LANES : (b + 1) * LANES]
    send[...] = weight[...] * head[...][None]


def finish_kernel(order_row, heads, ordered, inject, local, through, out):
    rows, width = ordered.shape
    carry = jnp.sum(heads[...], axis=0)
    back = (order_row[...] == iota((rows, rows), 0)).astype(jnp.float32).astype(jnp.bfloat16)
    for b in range(width // LANES):
        at = pl.ds(b * LANES, LANES)
        total = local[:, at] + through[:, at] * carry[b : b + 1, :]
        value = ordered[:, at].astype(jnp.float32) + inject[:, at] * total
        out[:, at] = jnp.dot(
            back, value.astype(jnp.bfloat16), preferred_element_type=jnp.float32
        ).astype(jnp.bfloat16)


def body(
    upstream,
    saved,
    expert_ids,
    gates,
    weight_in,
    weight_out,
    spatial_rate,
    temporal_rate,
    scan_order,
):
    experts = lax.axis_size("expert")
    frames = lax.axis_size("frame")
    rows = upstream.shape[1]
    width = upstream.shape[2]
    hidden_width = weight_in.shape[2]
    capacity = 2 * TOPK * rows // experts
    slots = experts * capacity
    blocks = width // LANES
    f32, bf16 = jnp.float32, jnp.bfloat16
    shape = jax.ShapeDtypeStruct
    me = lax.axis_index("expert")

    saved_all = lax.all_gather(saved[0], "expert", axis=0, tiled=True)

    ids_col = expert_ids[0]
    ids_row = ids_col.T
    rate = spatial_rate[0]
    info = call(
        info_kernel,
        shape((experts, blocks + 8, LANES), f32),
        "info",
        scratch_shapes=[pltpu.VMEM((blocks, LANES), f32)],
    )(ids_col, rate)
    got_info = lax.all_to_all(info, "expert", split_axis=0, concat_axis=0, tiled=True)
    send_routed = call(send_kernel, shape((slots, width), bf16), "send")(
        ids_row, gates[0].T, upstream[0]
    )
    routed_all = lax.all_to_all(
        send_routed.reshape(experts, capacity, width),
        "expert",
        split_axis=0,
        concat_axis=0,
        tiled=True,
    ).reshape(slots, width)

    local_order = scan_order - me * rows
    undo, ordered = call(
        order_kernel, (shape((rows, slots), bf16), shape((rows, width), bf16)), "order"
    )(ids_col, local_order.reshape(rows, 1), upstream[0])
    c1, c2, c4, cross, through = call(
        decay_kernel, (shape((rows, width), f32),) * 5, "decay"
    )(rate)
    inject = jnp.sqrt(-jnp.expm1(-2.0 * rate.astype(f32)))
    weights = [None] * experts
    weight = jnp.zeros((blocks, LANES), f32)
    for e in reversed(range(experts)):
        if e + 1 < experts:
            weight = weight * got_info[e + 1, :blocks]
        weight = jnp.where(e == me - 1, 1.0, weight)
        weights[e] = weight
    weight = jnp.stack(weights, axis=0)
    own_rate = lax.dynamic_slice_in_dim(
        temporal_rate, lax.axis_index("frame") * (width // frames), width // frames, axis=1
    )
    keep_time = jnp.exp(-own_rate)
    inject_time = jnp.sqrt(-jnp.expm1(-2.0 * own_rate))

    inputs_all = call(
        gather_kernel,
        shape((slots, width), bf16),
        "gather",
        grid=(experts,),
        in_specs=[
            pl.BlockSpec((1, blocks + 8, LANES), lambda i: (i, 0, 0)),
            pl.BlockSpec((rows, width), lambda i: (i, 0)),
        ],
        out_specs=pl.BlockSpec((capacity, width), lambda i: (i, 0)),
    )(got_info, saved_all)

    weight_in_one = weight_in[0]
    weight_out_one = weight_out[0]
    scale = 1.0 / math.sqrt(rows * experts * frames * upstream.shape[0])
    pre = jnp.dot(inputs_all, weight_in_one, preferred_element_type=f32)
    value, slope = gelu_parts(pre)
    hidden = value.astype(bf16)
    back_hidden = jnp.dot(routed_all, weight_out_one, preferred_element_type=f32)
    back_pre = (back_hidden * slope).astype(bf16)
    back_slots = lax.dot_general(
        back_pre, weight_in_one, (((1,), (1,)), ((), ())), preferred_element_type=f32
    ).astype(bf16)
    returned = lax.all_to_all(
        back_slots.reshape(experts, capacity, width),
        "expert",
        split_axis=0,
        concat_axis=0,
        tiled=True,
    ).reshape(slots, width)
    partial = (
        jnp.concatenate(
            [column_product(inputs_all, back_pre), column_product(routed_all, hidden)], axis=1
        )
        * scale
    ).astype(bf16)
    weight_rows = lax.psum_scatter(partial, "frame", scatter_dimension=0, tiled=True)
    grad_in = weight_rows[:, :hidden_width][None]
    grad_out = weight_rows[:, hidden_width:][None]

    mixed = call(undo_kernel, shape((blocks, rows, LANES), bf16), "undo")(undo, returned)
    pencil = lax.all_to_all(mixed, "frame", split_axis=0, concat_axis=0, tiled=True)
    pencil = call(temporal_kernel, shape(pencil.shape, bf16), "temporal")(
        pencil, keep_time, inject_time
    )
    spatial = lax.all_to_all(pencil, "frame", split_axis=0, concat_axis=0, tiled=True)
    local, heads = call(
        scan_kernel,
        (shape((rows, width), f32), shape((experts, blocks, LANES), f32)),
        "scan",
        scratch_shapes=[pltpu.VMEM((blocks, LANES), f32)],
    )(spatial, rate, weight, c1, c2, c4, cross)
    heads = lax.all_to_all(heads, "expert", split_axis=0, concat_axis=0, tiled=True)
    result = call(finish_kernel, shape((rows, width), bf16), "finish")(
        local_order.reshape(1, rows), heads, ordered, inject, local, through
    )
    return (result[None], grad_in, grad_out)


def solution(mesh):
    in_specs = (
        P("frame", "expert", None),
        P("frame", "expert", None),
        P("frame", "expert", None),
        P("frame", "expert", None),
        P("expert", None, None),
        P("expert", None, None),
        P("frame", "expert", None),
        P(),
        P("expert"),
    )
    out_specs = (P("frame", "expert", None), P("expert", "frame", None), P("expert", "frame", None))
    return jax.shard_map(body, mesh=mesh, in_specs=in_specs, out_specs=out_specs, check_vma=False)
```

profile of v0, /device:TPU:1, one launch (start us, length us, event | category | flops | bytes accessed | tf_op | source)
XLA Modules:
  0.0 293.0 jit_solution(8103532933511190976)
XLA Ops:
  10.8 10.0 %all-to-all-start.1 = ((f32[16,24,128]{2,1,0:T(8,128)}), f32[16,24,128]{2,1,0:T(8,128)S(1)}, u32[]{:S(2)}, u32[]{:S(2)}) async-start(f32[16,24,128]{2,1,0:T(8,128)} %info.1), calls=%async_computation.1 | async-start | bytes 393216 | tf_op jit(solution)/shard_map/all_to_all | solution.py:253
  21.6 2.3 send.1
  23.9 7.2 %all-to-all-done.1.info = f32[16,24,128]{2,1,0:T(8,128)S(1)} async-done(((f32[16,24,128]{2,1,0:T(8,128)}), f32[16,24,128]{2,1,0:T(8,128)S(1)}, u32[]{:S(2)}, u32[]{:S(2)}) %all-to-all-start.1) | async-done | bytes 196640 | tf_op jit(solution)/shard_map/all_to_all | solution.py:253
  31.1 4.3 %all-to-all-start = ((bf16[16,32,2048]{2,1,0:T(8,128)(2,1)}), bf16[16,32,2048]{2,1,0:T(8,128)(2,1)}, u32[]{:S(2)}, u32[]{:S(2)}) async-start(bf16[16,32,2048]{2,1,0:T(8,128)(2,1)} %bitcast.7), calls=%async_computation | async-start | bytes 4194304 | tf_op jit(solution)/shard_map/all_to_all | solution.py:257
  35.5 80.2 %all-gather.3.cloned.1.call-done = bf16[1,2048,2048]{2,1,0:T(8,128)(2,1)} async-done(((bf16[1,128,2048]{2,1,0:T(8,128)(2,1)}), bf16[1,2048,2048]{2,1,0:T(8,128)(2,1)}) %all-gather.3.cloned.1.call-update) | async-done | bytes 8388624 | tf_op jit(solution)/shard_map/all_gather | solution.py:242
  115.7 11.1 %gather.1 = bf16[512,2048]{1,0:T(8,128)(2,1)S(1)} custom-call(f32[16,24,128]{2,1,0:T(8,128)S(1)} %all-to-all-done.1.info, bf16[2048,2048]{1,0:T(8,128)(2,1)} %bitcast.50), custom_call_target="tpu_custom_call" | custom-call | tf_op jit(solution)/shard_map/gather/pallas_call | solution.py:287
  126.8 3.7 %fusion.3 = f32[512,1024]{1,0:T(8,128)} fusion(bf16[512,2048]{1,0:T(8,128)(2,1)S(1)} %gather.1, bf16[1,2048,1024]{2,1,0:T(8,128)(2,1)S(1)} %copy-done.21), kind=kOutput, calls=%fused_computation.4 | convolution fusion | flops 2147483648 | bytes 8388608 | tf_op jit(solution)/shard_map/dot_general | solution.py:302
  130.5 5.0 %fusion.19 = f32[2048,1024]{0,1:T(8,128)S(1)} fusion(bf16[512,2048]{1,0:T(8,128)(2,1)} %bitcast.8, f32[512,1024]{1,0:T(8,128)} %fusion.3), kind=kOutput, calls=%fused_computation.19 | convolution fusion | flops 2152202240 | bytes 12582912 | tf_op jit(solution)/shard_map/dot_general | solution.py:31
  135.5 4.9 %fusion.16 = bf16[512,1024]{1,0:T(8,128)(2,1)S(1)} fusion(f32[512,1024]{1,0:T(8,128)S(1)} %copy-done.24, bf16[512,2048]{1,0:T(8,128)(2,1)} %bitcast.8, bf16[1,2048,1024]{2,1,0:T(8,128)(2,1)S(1)} %copy-done.20), kind=kOutput, calls=%fused_computation.17 | convolution fusion | flops 2157445120 | bytes 9437184 | tf_op jit(solution)/shard_map/dot_general | solution.py:305
  141.4 2.5 fusion.51
  144.0 4.8 %fusion = bf16[2048,2048]{0,1:T(8,128)(2,1)} fusion(f32[2048,1024]{0,1:T(8,128)S(1)} %fusion.19, f32[2048,1024]{0,1:T(8,128)S(1)} %fusion.51), kind=kLoop, calls=%fused_computation.1 | loop fusion | flops 12582912 | bytes 25165824 | tf_op jit(solution)/shard_map/convert_element_type | solution.py:322
  148.8 12.3 %copy.22 = bf16[2048,2048]{1,0:T(8,128)(2,1)} copy(bf16[2048,2048]{0,1:T(8,128)(2,1)} %fusion) | data formatting | bytes 16777216
  162.4 5.9 %fusion.7 = bf16[512,2048]{1,0:T(8,128)(2,1)} fusion(bf16[512,1024]{1,0:T(8,128)(2,1)S(1)} %copy-done.23, bf16[1,2048,1024]{2,1,0:T(8,128)(2,1)} %param.13), kind=kOutput, calls=%fused_computation.10 | convolution fusion | flops 2148532224 | bytes 7340032 | tf_op jit(solution)/shard_map/dot_general | solution.py:307
  168.2 4.5 %all-to-all-start.2 = ((bf16[16,32,2048]{2,1,0:T(8,128)(2,1)}), bf16[16,32,2048]{2,1,0:T(8,128)(2,1)S(1)}, u32[]{:S(2)}, u32[]{:S(2)}) async-start(bf16[16,32,2048]{2,1,0:T(8,128)(2,1)} %bitcast.51), calls=%async_computation.2 | async-start | bytes 4194304 | tf_op jit(solution)/shard_map/all_to_all | solution.py:310
  172.7 1.4 decay.1
  182.1 39.6 %all-to-all-done.2 = bf16[16,32,2048]{2,1,0:T(8,128)(2,1)S(1)} async-done(((bf16[16,32,2048]{2,1,0:T(8,128)(2,1)}), bf16[16,32,2048]{2,1,0:T(8,128)(2,1)S(1)}, u32[]{:S(2)}, u32[]{:S(2)}) %all-to-all-start.2) | async-done | bytes 2097184 | tf_op jit(solution)/shard_map/all_to_all | solution.py:310
  223.8 6.9 %all-to-all-start.3 = ((bf16[16,128,128]{2,1,0:T(8,128)(2,1)}), bf16[16,128,128]{2,1,0:T(8,128)(2,1)S(1)}, u32[]{:S(2)}, u32[]{:S(2)}) async-start(bf16[16,128,128]{2,1,0:T(8,128)(2,1)} %undo.1), calls=%async_computation.3 | async-start | bytes 1048576 | tf_op jit(solution)/shard_map/all_to_all | solution.py:328
  230.8 10.3 %all-to-all-done.3.pencil = bf16[16,128,128]{2,1,0:T(8,128)(2,1)S(1)} async-done(((bf16[16,128,128]{2,1,0:T(8,128)(2,1)}), bf16[16,128,128]{2,1,0:T(8,128)(2,1)S(1)}, u32[]{:S(2)}, u32[]{:S(2)}) %all-to-all-start.3) | async-done | bytes 524320 | tf_op jit(solution)/shard_map/all_to_all | solution.py:328
  242.0 5.4 %all-to-all-start.4 = ((bf16[16,128,128]{2,1,0:T(8,128)(2,1)}), bf16[16,128,128]{2,1,0:T(8,128)(2,1)S(1)}, u32[]{:S(2)}, u32[]{:S(2)}) async-start(bf16[16,128,128]{2,1,0:T(8,128)(2,1)} %temporal.1), calls=%async_computation.4 | async-start | bytes 1048576 | tf_op jit(solution)/shard_map/all_to_all | solution.py:332
  247.5 8.9 %all-to-all-done.4.spatial = bf16[16,128,128]{2,1,0:T(8,128)(2,1)S(1)} async-done(((bf16[16,128,128]{2,1,0:T(8,128)(2,1)}), bf16[16,128,128]{2,1,0:T(8,128)(2,1)S(1)}, u32[]{:S(2)}, u32[]{:S(2)}) %all-to-all-start.4) | async-done | bytes 524320 | tf_op jit(solution)/shard_map/all_to_all | solution.py:332
  258.8 2.4 scan.1
  262.2 9.2 %all-to-all-start.5 = ((f32[16,16,128]{2,1,0:T(8,128)}), f32[16,16,128]{2,1,0:T(8,128)S(1)}, u32[]{:S(2)}, u32[]{:S(2)}) async-start(f32[16,16,128]{2,1,0:T(8,128)} %get-tuple-element.17), calls=%async_computation.5 | async-start | bytes 262144 | tf_op jit(solution)/shard_map/all_to_all | solution.py:339
  272.0 8.5 %all-to-all-done.5.heads = f32[16,16,128]{2,1,0:T(8,128)S(1)} async-done(((f32[16,16,128]{2,1,0:T(8,128)}), f32[16,16,128]{2,1,0:T(8,128)S(1)}, u32[]{:S(2)}, u32[]{:S(2)}) %all-to-all-start.5) | async-done | bytes 131104 | tf_op jit(solution)/shard_map/all_to_all | solution.py:339
  281.8 1.3 finish.1
  (87 shorter events, 26.1 us)
Async XLA Ops:
  7.2 13.7 %copy-start.2 = (bf16[1,128,2048]{2,1,0:T(8,128)(2,1)S(1)}, bf16[1,128,2048]{2,1,0:T(8,128)(2,1)}, u32[]{:S(2)}) copy-start(bf16[1,128,2048]{2,1,0:T(8,128)(2,1)} %param.9) | copy-start | bytes 1572868
  7.2 108.5 %all-gather.3.cloned.1.call-start = ((), (), s32[]{:S(2)}) async-start(), calls=%async_computation.7 | async-start | bytes 8912896 | tf_op jit(solution)/shard_map/all_gather | solution.py:242
  8.7 1.0 copy-start
  10.8 20.2 %all-to-all-start.1 = ((f32[16,24,128]{2,1,0:T(8,128)}), f32[16,24,128]{2,1,0:T(8,128)S(1)}, u32[]{:S(2)}, u32[]{:S(2)}) async-start(f32[16,24,128]{2,1,0:T(8,128)} %info.1), calls=%async_computation.1 | async-start | bytes 393216 | tf_op jit(solution)/shard_map/all_to_all | solution.py:253
  31.1 99.4 %all-to-all-start = ((bf16[16,32,2048]{2,1,0:T(8,128)(2,1)}), bf16[16,32,2048]{2,1,0:T(8,128)(2,1)}, u32[]{:S(2)}, u32[]{:S(2)}) async-start(bf16[16,32,2048]{2,1,0:T(8,128)(2,1)} %bitcast.7), calls=%async_computation | async-start | bytes 4194304 | tf_op jit(solution)/shard_map/all_to_all | solution.py:257
  35.4 247.6 %reduce-scatter.4.cloned.1.call-start = ((), (), s32[]{:S(2)}) async-start(), calls=%async_computation.8 | async-start | bytes 8912896
  115.7 11.1 %copy-start.21 = (bf16[1,2048,1024]{2,1,0:T(8,128)(2,1)S(1)}, bf16[1,2048,1024]{2,1,0:T(8,128)(2,1)}, u32[]{:S(2)}) copy-start(bf16[1,2048,1024]{2,1,0:T(8,128)(2,1)} %param.13) | copy-start | bytes 12582916
  130.5 5.1 %copy-start.20 = (bf16[1,2048,1024]{2,1,0:T(8,128)(2,1)S(1)}, bf16[1,2048,1024]{2,1,0:T(8,128)(2,1)}, u32[]{:S(2)}) copy-start(bf16[1,2048,1024]{2,1,0:T(8,128)(2,1)} %param.14) | copy-start | bytes 12582916
  130.5 5.1 %copy-start.24 = (f32[512,1024]{1,0:T(8,128)S(1)}, f32[512,1024]{1,0:T(8,128)}, u32[]{:S(2)}) copy-start(f32[512,1024]{1,0:T(8,128)} %fusion.3) | copy-start | bytes 6291460
  140.4 1.0 copy-start.22
  161.1 1.2 copy-start.23
  168.2 4.5 %copy-start.1 = (bf16[1,128,2048]{2,1,0:T(8,128)(2,1)S(1)}, bf16[1,128,2048]{2,1,0:T(8,128)(2,1)}, u32[]{:S(2)}) copy-start(bf16[1,128,2048]{2,1,0:T(8,128)(2,1)} %param.15) | copy-start | bytes 1572868
  168.2 10.8 %copy-start.19 = (s32[128]{0:T(128)S(1)}, s32[128]{0:T(128)}, u32[]{:S(2)}) copy-start(s32[128]{0:T(128)} %param.17) | copy-start | bytes 1540
  168.2 53.4 %all-to-all-start.2 = ((bf16[16,32,2048]{2,1,0:T(8,128)(2,1)}), bf16[16,32,2048]{2,1,0:T(8,128)(2,1)S(1)}, u32[]{:S(2)}, u32[]{:S(2)}) async-start(bf16[16,32,2048]{2,1,0:T(8,128)(2,1)} %bitcast.51), calls=%async_computation.2 | async-start | bytes 4194304 | tf_op jit(solution)/shard_map/all_to_all | solution.py:310
  175.1 1.0 copy-start.7
  223.8 32.6 %copy-start.8 = (f32[128,2048]{1,0:T(8,128)S(1)}, f32[128,2048]{1,0:T(8,128)}, u32[]{:S(2)}) copy-start(f32[128,2048]{1,0:T(8,128)} %copy-done.7) | copy-start | bytes 3145732
  223.8 17.2 %all-to-all-start.3 = ((bf16[16,128,128]{2,1,0:T(8,128)(2,1)}), bf16[16,128,128]{2,1,0:T(8,128)(2,1)S(1)}, u32[]{:S(2)}, u32[]{:S(2)}) async-start(bf16[16,128,128]{2,1,0:T(8,128)(2,1)} %undo.1), calls=%async_computation.3 | async-start | bytes 1048576 | tf_op jit(solution)/shard_map/all_to_all | solution.py:328
  242.0 14.4 %all-to-all-start.4 = ((bf16[16,128,128]{2,1,0:T(8,128)(2,1)}), bf16[16,128,128]{2,1,0:T(8,128)(2,1)S(1)}, u32[]{:S(2)}, u32[]{:S(2)}) async-start(bf16[16,128,128]{2,1,0:T(8,128)(2,1)} %temporal.1), calls=%async_computation.4 | async-start | bytes 1048576 | tf_op jit(solution)/shard_map/all_to_all | solution.py:332
  256.4 1.2 copy-start.10
  257.6 1.2 copy-start.12
  262.2 18.3 %copy-start.4 = (f32[128,2048]{1,0:T(8,128)S(1)}, f32[128,2048]{1,0:T(8,128)}, u32[]{:S(2)}) copy-start(f32[128,2048]{1,0:T(8,128)} %copy-done.3) | copy-start | bytes 3145732
  262.2 18.3 %copy-start.15 = (bf16[128,2048]{1,0:T(8,128)(2,1)S(1)}, bf16[128,2048]{1,0:T(8,128)(2,1)}, u32[]{:S(2)}) copy-start(bf16[128,2048]{1,0:T(8,128)(2,1)} %copy-done.14) | copy-start | bytes 1572868
  262.2 18.3 %all-to-all-start.5 = ((f32[16,16,128]{2,1,0:T(8,128)}), f32[16,16,128]{2,1,0:T(8,128)S(1)}, u32[]{:S(2)}, u32[]{:S(2)}) async-start(f32[16,16,128]{2,1,0:T(8,128)} %get-tuple-element.17), calls=%async_computation.5 | async-start | bytes 262144 | tf_op jit(solution)/shard_map/all_to_all | solution.py:339
  280.6 1.2 copy-start.6
  (9 other events, 7.9 us)
Sparse Core Ops, SparseCore 0:
  9.8 105.7 all-gather.2
  161.3 90.1 reduce-scatter.3
where the time goes:
time: 294 us; the launch traced here: 293 us
  waiting for transfers between devices  155 us (53%)
  starting transfers between devices  40.3 us (14%)
  local copies, waits for them, and re-layouts  32.3 us (11%)
  Pallas kernels  22.4 us (8%)
  matrix products  22 us (7%)
  between operations  14.3 us (5%)
  other arithmetic  6.23 us (2%)
    all_gather x1, waiting for transfers between devices, body(): saved_all = lax.all_gather(saved[0], 'expert', axis=0, tiled=True)  80.2 us
    all_to_all x1, waiting for transfers between devices, body(): lax.all_to_all(back_slots.reshape(experts, capacity, width), 'expert', sp...  39.6 us
    unnamed x63, local copies, waits for them, and re-layouts  31.1 us
    pallas_call x1, Pallas kernels, body(): call(gather_kernel, shape((slots, width), bf16), 'gather', grid=(experts,...  11.1 us
    all_to_all x1, waiting for transfers between devices, body(): lax.all_to_all(mixed, 'frame', split_axis=0, concat_axis=0, tiled=True)  10.3 us
    all_to_all x1, starting transfers between devices, body(): lax.all_to_all(info, 'expert', split_axis=0, concat_axis=0, tiled=True)  9.98 us
    all_to_all x1, starting transfers between devices, body(): lax.all_to_all(heads, 'expert', split_axis=0, concat_axis=0, tiled=True)  9.16 us
    all_to_all x1, waiting for transfers between devices, body(): lax.all_to_all(pencil, 'frame', split_axis=0, concat_axis=0, tiled=True)  8.91 us
  transfers between devices with their start and end apart: 8, of which 6 were waited for; matrix products, arithmetic and copies ran while one was open for 4% of the time, Pallas kernels for 7%

commit v1 on v0

--- a/solution.py
+++ b/solution.py
@@ -47,55 +47,177 @@
     )
 
 
-def info_kernel(ids_col, rate, info, head):
+def info_kernel(facts, rate, info, head):
     experts = info.shape[0]
-    rows, width = rate.shape
-    blocks = width // LANES
-    slots = experts * 32
-    expert_of = iota((rows, slots), 1) // 32
-    slot_of = iota((rows, slots), 1) % 32
-    token = iota((rows, slots), 0)
-    hit = (ids_col[:, 0:1] == expert_of) | (ids_col[:, 1:2] == expert_of)
-    before = (iota((rows, rows), 1) < iota((rows, rows), 0)).astype(jnp.bfloat16)
-    rank = jnp.dot(
-        before, hit.astype(jnp.float32).astype(jnp.bfloat16), preferred_element_type=jnp.float32
-    )
-    chosen = hit & (rank.astype(jnp.int32) == slot_of)
-    row_of = (
-        jnp.sum(jnp.where(chosen, (token + 1).astype(jnp.float32), 0.0), axis=0, keepdims=True) - 1.0
-    )
+    blocks = rate.shape[1] // LANES
     total = jnp.exp(-jnp.sum(rate[...].astype(jnp.float32), axis=0, keepdims=True))
     for b in range(blocks):
         head[b : b + 1, :] = total[:, b * LANES : (b + 1) * LANES]
     spread = head[...]
     for e in range(experts):
         info[e, 0:blocks, :] = spread
-        info[e, blocks : blocks + 8, :] = jnp.zeros((8, LANES), jnp.float32)
-        info[e, blocks : blocks + 1, 0:32] = row_of[:, e * 32 : (e + 1) * 32]
-
-
-def send_kernel(ids_row, gates_row, upstream, send):
-    slots = send.shape[0]
-    rows, width = upstream.shape
-    expert_of = iota((slots, rows), 0) // 32
-    slot_of = iota((slots, rows), 0) % 32
-    first = ids_row[0:1, :] == expert_of
-    hit = first | (ids_row[1:2, :] == expert_of)
-    before = (iota((rows, rows), 0) < iota((rows, rows), 1)).astype(jnp.bfloat16)
+        info[e, blocks : blocks + 4, :] = facts[...]
+        info[e, blocks + 4 : blocks + 8, :] = jnp.zeros((4, LANES), jnp.float32)
+
+
+def chosen_rows(info, source, experts, x, gated, put):
+    rows, width = x.shape
+    slots = 32 * len(experts)
+    ids = [info[source, 16 + k : 17 + k, :] for k in range(TOPK)]
+    expert_of = jnp.concatenate([jnp.full((32, rows), e, jnp.int32) for e in experts], axis=0)
+    expert_of = expert_of.astype(jnp.float32)
+    slot_of = (iota((slots, rows), 0) % 32).astype(jnp.float32)
+    first = ids[0] == expert_of
+    hit = first | (ids[1] == expert_of)
+    before = (iota((rows, rows), 0) < iota((rows, rows), 1)).astype(jnp.float32)
     rank = jnp.dot(
-        hit.astype(jnp.float32).astype(jnp.bfloat16), before, preferred_element_type=jnp.float32
-    )
-    chosen = hit & (rank.astype(jnp.int32) == slot_of)
-    gate = jnp.sum(
-        jnp.where(chosen, jnp.where(first, gates_row[0:1, :], gates_row[1:2, :]), 0.0),
-        axis=1,
-        keepdims=True,
-    )
+        hit.astype(jnp.float32).astype(jnp.bfloat16),
+        before.astype(jnp.bfloat16),
+        preferred_element_type=jnp.float32,
+    )
+    chosen = hit & (rank == slot_of)
     pick = chosen.astype(jnp.float32).astype(jnp.bfloat16)
+    if gated:
+        gate = jnp.where(first, info[source, 18:19, :], info[source, 19:20, :])
+        gate = jnp.sum(jnp.where(chosen, gate, 0.0), axis=1, keepdims=True)
     step = 512
     for c in range(0, width, step):
-        part = jnp.dot(pick, upstream[:, c : c + step], preferred_element_type=jnp.float32)
-        send[:, c : c + step] = (gate * part).astype(jnp.bfloat16)
+        part = jnp.dot(pick, x[:, c : c + step], preferred_element_type=jnp.float32)
+        if gated:
+            part = gate * part
+        put(c, step, part.astype(jnp.bfloat16))
+
+
+def pack_kernel(gated, me, info, up, down, pack_up, pack_down):
+    e = me[0]
+    z, core = e // 2, e % 2
+    at = lambda n: (n + 16) % 16
+
+    def put_in(out):
+        def put(c, step, part):
+            out[:, c : c + step] = part
+
+        return put
+
+    chosen_rows(
+        info,
+        at(e - 4),
+        [at(2 * z + 2), at(2 * z + 3), at(2 * z + 4)],
+        up,
+        gated,
+        put_in(pack_up),
+    )
+    chosen_rows(
+        info,
+        at(e + 4),
+        [at(2 * z - 2), at(2 * z - 1), at(2 * z - 3)],
+        down,
+        gated,
+        put_in(pack_down),
+    )
+
+
+NEAR = (0, -1, -2, 1, 2)
+FAR = (-3, 3, 4)
+
+
+def near_kernel(gated, me, info, *refs):
+    sources, (own, other) = refs[:5], refs[5:]
+    e = me[0]
+    z, core = e // 2, e % 2
+    for i, away in enumerate(NEAR):
+
+        def put(c, step, part):
+            own[32 * i : 32 * i + 32, c : c + step] = part[0:32]
+            other[32 * i : 32 * i + 32, c : c + step] = part[32:64]
+
+        chosen_rows(
+            info, (e + 2 * away + 16) % 16, [e, 2 * z + 1 - core], sources[i], gated, put
+        )
+
+
+def far_kernel(me, up3, down3, up4, down4, own, other):
+    core = me[0] % 2
+    mine = pl.ds(pl.multiple_of(core * 32, 32), 32)
+    theirs = pl.ds(pl.multiple_of(32 - core * 32, 32), 32)
+    own[0:32, :] = up3[mine, :]
+    other[0:32, :] = up3[theirs, :]
+    own[32:64, :] = down3[mine, :]
+    other[32:64, :] = down3[theirs, :]
+
+    @pl.when(core == 0)
+    def _():
+        own[64:96, :] = up4[...]
+        other[64:96, :] = down4[...]
+
+    @pl.when(core == 1)
+    def _():
+        own[64:96, :] = down4[...]
+        other[64:96, :] = up4[...]
+
+
+def join(pieces, out):
+    at = 0
+    for piece in pieces:
+        out[at : at + piece.shape[0], :] = piece[...]
+        at += piece.shape[0]
+
+
+def forward_kernel(own1, own2, got1, got2, weight_in, inputs, hidden, slope):
+    join((own1, own2, got1, got2), inputs)
+    step = 256
+
+    def part(n, _):
+        at = pl.ds(pl.multiple_of(n * step, step), step)
+        pre = jnp.dot(inputs[...], weight_in[:, at], preferred_element_type=jnp.float32)
+        value, rise = gelu_parts(pre)
+        hidden[:, at] = value.astype(jnp.bfloat16)
+        slope[:, at] = rise
+        return 0
+
+    lax.fori_loop(0, hidden.shape[1] // step, part, 0)
+
+
+def backward_kernel(
+    me, own1, own2, got1, got2, weight_out, weight_in, slope, routed, back_pre, back
+):
+    join((own1, own2, got1, got2), routed)
+    step = 256
+
+    def part(n, _):
+        at = pl.ds(pl.multiple_of(n * step, step), step)
+        back_hidden = jnp.dot(routed[...], weight_out[:, at], preferred_element_type=jnp.float32)
+        back_pre[:, at] = (back_hidden * slope[:, at]).astype(jnp.bfloat16)
+        return 0
+
+    lax.fori_loop(0, back_pre.shape[1] // step, part, 0)
+    e = me[0]
+    z, core = e // 2, e % 2
+    targets = []
+    for owner in (core, 1 - core):
+        targets += [2 * ((z + away + 8) % 8) + owner for away in NEAR + FAR]
+
+    def route(n, _):
+        at = pl.ds(pl.multiple_of(n * step, step), step)
+        rows = lax.dot_general(
+            back_pre[...],
+            weight_in[at, :],
+            (((1,), (1,)), ((), ())),
+            preferred_element_type=jnp.float32,
+        ).astype(jnp.bfloat16)
+        for i, target in enumerate(targets):
+            back[target, :, at] = rows[32 * i : 32 * i + 32]
+        return 0
+
+    lax.fori_loop(0, weight_in.shape[0] // step, route, 0)
+
+
+def grads_kernel(scale, inputs, routed, back_pre, hidden, out):
+    half = back_pre.shape[1]
+    out[:, 0:half] = (column_product(inputs[...], back_pre[...]) * scale).astype(jnp.bfloat16)
+    out[:, half : 2 * half] = (column_product(routed[...], hidden[...]) * scale).astype(
+        jnp.bfloat16
+    )
 
 
 def order_kernel(ids_col, order_col, upstream, undo, ordered):
@@ -146,18 +268,6 @@
     lax.fori_loop(0, width // LANES, column, 0)
 
 
-def gather_kernel(info, saved, picked):
-    rows = saved.shape[0]
-    row_of = info[0, 16:17, 0:32]
-    pick = (iota((rows, 32), 0).astype(jnp.float32) == row_of).astype(jnp.float32)
-    picked[...] = lax.dot_general(
-        pick.astype(jnp.bfloat16),
-        saved[...],
-        (((0,), (0,)), ((), ())),
-        preferred_element_type=jnp.float32,
-    ).astype(jnp.bfloat16)
-
-
 def undo_kernel(undo, returned, mixed):
     blocks = mixed.shape[0]
     pick = undo[...]
@@ -239,28 +349,55 @@
     shape = jax.ShapeDtypeStruct
     me = lax.axis_index("expert")
 
-    saved_all = lax.all_gather(saved[0], "expert", axis=0, tiled=True)
+    up = [(i, (i + 2) % experts) for i in range(experts)]
+    down = [(i, (i - 2) % experts) for i in range(experts)]
+    swap = [(i, i ^ 1) for i in range(experts)]
+    scalar = me.astype(jnp.int32).reshape(1)
+    smem = pl.BlockSpec(memory_space=pltpu.SMEM)
+    vmem = pl.BlockSpec(memory_space=pltpu.VMEM)
 
     ids_col = expert_ids[0]
-    ids_row = ids_col.T
     rate = spatial_rate[0]
+    facts = jnp.concatenate([ids_col.T.astype(f32), gates[0].T], axis=0)
+    chains = []
+    for x in (saved[0], upstream[0]):
+        up1, down1 = lax.ppermute(x, "expert", up), lax.ppermute(x, "expert", down)
+        chains.append([x, up1, down1])
     info = call(
         info_kernel,
         shape((experts, blocks + 8, LANES), f32),
         "info",
         scratch_shapes=[pltpu.VMEM((blocks, LANES), f32)],
-    )(ids_col, rate)
+    )(facts, rate)
     got_info = lax.all_to_all(info, "expert", split_axis=0, concat_axis=0, tiled=True)
-    send_routed = call(send_kernel, shape((slots, width), bf16), "send")(
-        ids_row, gates[0].T, upstream[0]
-    )
-    routed_all = lax.all_to_all(
-        send_routed.reshape(experts, capacity, width),
-        "expert",
-        split_axis=0,
-        concat_axis=0,
-        tiled=True,
-    ).reshape(slots, width)
+    pieces = []
+    for gated, (x, up1, down1) in enumerate(chains):
+        up2, down2 = lax.ppermute(up1, "expert", up), lax.ppermute(down1, "expert", down)
+        packed = call(
+            functools.partial(pack_kernel, bool(gated)),
+            (shape((96, width), bf16),) * 2,
+            "pack",
+            in_specs=[smem] + [vmem] * 3,
+        )(scalar, got_info, up2, down2)
+        up3 = lax.ppermute(packed[0], "expert", up)
+        down3 = lax.ppermute(packed[1], "expert", down)
+        up4 = lax.ppermute(up3[64:96], "expert", up)
+        down4 = lax.ppermute(down3[64:96], "expert", down)
+        own1, other1 = call(
+            functools.partial(near_kernel, bool(gated)),
+            (shape((160, width), bf16),) * 2,
+            "near",
+            in_specs=[smem] + [vmem] * 6,
+        )(scalar, got_info, x, up1, up2, down1, down2)
+        got1 = lax.ppermute(other1, "expert", swap)
+        own2, other2 = call(
+            far_kernel,
+            (shape((96, width), bf16),) * 2,
+            "far",
+            in_specs=[smem] + [vmem] * 4,
+        )(scalar, up3, down3, up4, down4)
+        got2 = lax.ppermute(other2, "expert", swap)
+        pieces.append((own1, own2, got1, got2))
 
     local_order = scan_order - me * rows
     undo, ordered = call(
@@ -284,42 +421,45 @@
     keep_time = jnp.exp(-own_rate)
     inject_time = jnp.sqrt(-jnp.expm1(-2.0 * own_rate))
 
-    inputs_all = call(
-        gather_kernel,
-        shape((slots, width), bf16),
-        "gather",
-        grid=(experts,),
-        in_specs=[
-            pl.BlockSpec((1, blocks + 8, LANES), lambda i: (i, 0, 0)),
-            pl.BlockSpec((rows, width), lambda i: (i, 0)),
-        ],
-        out_specs=pl.BlockSpec((capacity, width), lambda i: (i, 0)),
-    )(got_info, saved_all)
-
     weight_in_one = weight_in[0]
     weight_out_one = weight_out[0]
     scale = 1.0 / math.sqrt(rows * experts * frames * upstream.shape[0])
-    pre = jnp.dot(inputs_all, weight_in_one, preferred_element_type=f32)
-    value, slope = gelu_parts(pre)
-    hidden = value.astype(bf16)
-    back_hidden = jnp.dot(routed_all, weight_out_one, preferred_element_type=f32)
-    back_pre = (back_hidden * slope).astype(bf16)
-    back_slots = lax.dot_general(
-        back_pre, weight_in_one, (((1,), (1,)), ((), ())), preferred_element_type=f32
-    ).astype(bf16)
+    inputs_all, hidden, slope = call(
+        forward_kernel,
+        (
+            shape((slots, width), bf16),
+            shape((slots, hidden_width), bf16),
+            shape((slots, hidden_width), f32),
+        ),
+        "forward",
+    )(*pieces[0], weight_in_one)
+    routed_all, back_pre, back_slots = call(
+        backward_kernel,
+        (
+            shape((slots, width), bf16),
+            shape((slots, hidden_width), bf16),
+            shape((experts, capacity, width), bf16),
+        ),
+        "backward",
+        in_specs=[smem] + [vmem] * 7,
+    )(scalar, *pieces[1], weight_out_one, weight_in_one, slope)
     returned = lax.all_to_all(
-        back_slots.reshape(experts, capacity, width),
-        "expert",
-        split_axis=0,
-        concat_axis=0,
-        tiled=True,
+        back_slots, "expert", split_axis=0, concat_axis=0, tiled=True
     ).reshape(slots, width)
-    partial = (
-        jnp.concatenate(
-            [column_product(inputs_all, back_pre), column_product(routed_all, hidden)], axis=1
-        )
-        * scale
-    ).astype(bf16)
+    step = 256
+    partial = call(
+        functools.partial(grads_kernel, scale),
+        shape((width, 2 * hidden_width), bf16),
+        "grads",
+        grid=(width // step,),
+        in_specs=[
+            pl.BlockSpec((slots, step), lambda i: (0, i)),
+            pl.BlockSpec((slots, step), lambda i: (0, i)),
+            pl.BlockSpec((slots, hidden_width), lambda i: (0, 0)),
+            pl.BlockSpec((slots, hidden_width), lambda i: (0, 0)),
+        ],
+        out_specs=pl.BlockSpec((step, 2 * hidden_width), lambda i: (i, 0)),
+    )(inputs_all, routed_all, back_pre, hidden)
     weight_rows = lax.psum_scatter(partial, "frame", scatter_dimension=0, tiled=True)
     grad_in = weight_rows[:, :hidden_width][None]
     grad_out = weight_rows[:, hidden_width:][None]

time: 294 us -> 254 us (0.86)
  waiting for transfers between devices: 155 us -> 109 us
  starting transfers between devices: 40.3 us -> 64.3 us
  matrix products: 22 us -> 0 us
  Pallas kernels: 22.4 us -> 43.1 us
  local copies, waits for them, and re-layouts: 32.3 us -> 18.7 us
  other arithmetic: 6.23 us -> 2.8 us
    all_gather x1 -> x0, waiting for transfers between devices: 80.2 us -> none  [body(): saved_all = lax.all_gather(saved[0], 'expert', axis=0, tiled=True)]
    ppermute x0 -> x20, starting transfers between devices: none -> 30.8 us  [the longest x2 6.7 us: body(): lax.ppermute(x, 'expert', down)]
    ppermute x0 -> x20, waiting for transfers between devices: none -> 24.6 us  [the longest x2 17.1 us: body(): lax.ppermute(x, 'expert', up)]
    dot_general x5 -> x0, matrix products: 22 us -> none  [the longest x2 7.58 us: column_product(): lax.dot_general(left, right, (((0,), (0,)), ((), ())), preferred_element_...]
    pallas_call x2 -> x9, Pallas kernels: 13.4 us -> 34.4 us  [the longest x1 12.3 us: body(): call(backward_kernel, (shape((slots, width), bf16), shape((slots, hidden_...]
    unnamed x63 -> x59, local copies, waits for them, and re-layouts: 31.1 us -> 16.6 us
    all_to_all x1, waiting for transfers between devices: 7.18 us -> 14.1 us  [body(): lax.all_to_all(info, 'expert', split_axis=0, concat_axis=0, tiled=True)]
    convert_element_type x1, other arithmetic: 4.8 us -> 0.68 us  [body(): facts = jnp.concatenate([ids_col.T.astype(f32), gates[0].T], axis=0)]
  transfers between devices with their start and end apart: 8 -> 26, of which waited for: 6 -> 11; matrix products, arithmetic and copies ran while one was open for 4% -> 1% of each run, Pallas kernels for 7% -> 8%
where the time goes in v1:
time: 254 us; the launch traced here: 253 us
  waiting for transfers between devices  109 us (43%)
  starting transfers between devices  64.3 us (25%)
  Pallas kernels  43.1 us (17%)
  local copies, waits for them, and re-layouts  18.7 us (7%)
  between operations  14.4 us (6%)
  other arithmetic  2.8 us (1%)
    all_to_all x1, waiting for transfers between devices, body(): lax.all_to_all(back_slots, 'expert', split_axis=0, concat_axis=0, tiled=T...  39.3 us
    ppermute x2, waiting for transfers between devices, body(): lax.ppermute(x, 'expert', up)  17.1 us
    unnamed x59, local copies, waits for them, and re-layouts  16.6 us
    all_to_all x1, waiting for transfers between devices, body(): lax.all_to_all(info, 'expert', split_axis=0, concat_axis=0, tiled=True)  14.1 us
    all_to_all x1, waiting for transfers between devices, body(): lax.all_to_all(pencil, 'frame', split_axis=0, concat_axis=0, tiled=True)  12.5 us
    pallas_call x1, Pallas kernels, body(): call(backward_kernel, (shape((slots, width), bf16), shape((slots, hidden_...  12.3 us
    all_to_all x1, waiting for transfers between devices, body(): lax.all_to_all(mixed, 'frame', split_axis=0, concat_axis=0, tiled=True)  10.3 us
    pallas_call x1, Pallas kernels, body(): call(functools.partial(grads_kernel, scale), shape((width, 2 * hidden_wid...  9.6 us
  transfers between devices with their start and end apart: 26, of which 11 were waited for; matrix products, arithmetic and copies ran while one was open for 1% of the time, Pallas kernels for 8%

profile of v1, /device:TPU:1, one launch (start us, length us, event | category | flops | bytes accessed | tf_op | source)
XLA Modules:
  0.0 252.7 jit_solution(1002262169925991430)
XLA Ops:
  7.2 2.5 %collective-permute-start.10 = (bf16[128,2048]{1,0:T(8,128)(2,1)}, bf16[128,2048]{1,0:T(8,128)(2,1)S(1)}, u32[]{:S(2)}, u32[]{:S(2)}) collective-permute-start(bf16[128,2048]{1,0:T(8,128)(2,1)} %bitcast.32), channel_id=1, source_target_pairs={{0,2},{1,3},{2,4},{3,5},{4,6},{5,7},{6,8},{7,9},{8,10},{9,11},{10,... | collective-permute-start | bytes 1572872 | tf_op jit(solution)/shard_map/ppermute | solution.py:364
  9.7 4.0 %collective-permute-start.12 = (bf16[128,2048]{1,0:T(8,128)(2,1)}, bf16[128,2048]{1,0:T(8,128)(2,1)S(1)}, u32[]{:S(2)}, u32[]{:S(2)}) collective-permute-start(bf16[128,2048]{1,0:T(8,128)(2,1)} %bitcast.33), channel_id=1, source_target_pairs={{0,14},{1,15},{2,0},{3,1},{4,2},{5,3},{6,4},{7,5},{8,6},{9,7},{10,... | collective-permute-start | bytes 1572872 | tf_op jit(solution)/shard_map/ppermute | solution.py:364
  13.7 2.7 %collective-permute-start.2 = (bf16[128,2048]{1,0:T(8,128)(2,1)}, bf16[128,2048]{1,0:T(8,128)(2,1)}, u32[]{:S(2)}, u32[]{:S(2)}) collective-permute-start(bf16[128,2048]{1,0:T(8,128)(2,1)} %bitcast.29), channel_id=1, source_target_pairs={{0,14},{1,15},{2,0},{3,1},{4,2},{5,3},{6,4},{7,5},{8,6},{9,7},{10,... | collective-permute-start | bytes 1572872 | tf_op jit(solution)/shard_map/ppermute | solution.py:364
  16.4 9.1 %collective-permute-done.10.refs_1_ = bf16[128,2048]{1,0:T(8,128)(2,1)S(1)} collective-permute-done((bf16[128,2048]{1,0:T(8,128)(2,1)}, bf16[128,2048]{1,0:T(8,128)(2,1)S(1)}, u32[]{:S(2)}, u32[]{:S(2)}) %collective-permute-start.10) | collective-permute-done | bytes 524320 | tf_op jit(solution)/shard_map/ppermute | solution.py:364
  25.5 2.7 %collective-permute-start.13 = (bf16[128,2048]{1,0:T(8,128)(2,1)S(1)}, bf16[128,2048]{1,0:T(8,128)(2,1)S(1)}, u32[]{:S(2)}, u32[]{:S(2)}) collective-permute-start(bf16[128,2048]{1,0:T(8,128)(2,1)S(1)} %collective-permute-done.12.refs_3_), channel_id=1, source_target_pairs={{0,14},{1,15},{2,0},{3,1},{4,2},{5,3},{6,4},{7,5},{8,6},{9,7},{10,... | collective-permute-start | bytes 1572872 | tf_op jit(solution)/shard_map/ppermute | solution.py:375
  28.9 8.0 %collective-permute-done.refs_1_ = bf16[128,2048]{1,0:T(8,128)(2,1)} collective-permute-done((bf16[128,2048]{1,0:T(8,128)(2,1)}, bf16[128,2048]{1,0:T(8,128)(2,1)}, u32[]{:S(2)}, u32[]{:S(2)}) %collective-permute-start) | collective-permute-done | bytes 524320 | tf_op jit(solution)/shard_map/ppermute | solution.py:364
  36.9 2.7 %collective-permute-start.3 = (bf16[128,2048]{1,0:T(8,128)(2,1)}, bf16[128,2048]{1,0:T(8,128)(2,1)S(1)}, u32[]{:S(2)}, u32[]{:S(2)}) collective-permute-start(bf16[128,2048]{1,0:T(8,128)(2,1)} %collective-permute-done.2.refs_3_), channel_id=1, source_target_pairs={{0,14},{1,15},{2,0},{3,1},{4,2},{5,3},{6,4},{7,5},{8,6},{9,7},{10,... | collective-permute-start | bytes 1572872 | tf_op jit(solution)/shard_map/ppermute | solution.py:375
  42.1 8.5 %all-to-all-start = ((f32[16,24,128]{2,1,0:T(8,128)}), f32[16,24,128]{2,1,0:T(8,128)S(1)}, u32[]{:S(2)}, u32[]{:S(2)}) async-start(f32[16,24,128]{2,1,0:T(8,128)} %info.1), calls=%async_computation | async-start | bytes 393216 | tf_op jit(solution)/shard_map/all_to_all | solution.py:372
  50.7 14.1 %all-to-all-done.info = f32[16,24,128]{2,1,0:T(8,128)S(1)} async-done(((f32[16,24,128]{2,1,0:T(8,128)}), f32[16,24,128]{2,1,0:T(8,128)S(1)}, u32[]{:S(2)}, u32[]{:S(2)}) %all-to-all-start) | async-done | bytes 196640 | tf_op jit(solution)/shard_map/all_to_all | solution.py:372
  65.5 3.3 %collective-permute-start.14 = (bf16[96,2048]{1,0:T(8,128)(2,1)S(1)}, bf16[96,2048]{1,0:T(8,128)(2,1)S(1)}, u32[]{:S(2)}, u32[]{:S(2)}) collective-permute-start(bf16[96,2048]{1,0:T(8,128)(2,1)S(1)} %get-tuple-element.38), channel_id=1, source_target_pairs={{0,2},{1,3},{2,4},{3,5},{4,6},{5,7},{6,8},{7,9},{8,10},{9,11},{10,... | collective-permute-start | bytes 1179656 | tf_op jit(solution)/shard_map/ppermute | solution.py:382
  81.4 4.8 %collective-permute-done.4.up3 = bf16[96,2048]{1,0:T(8,128)(2,1)S(1)} collective-permute-done((bf16[96,2048]{1,0:T(8,128)(2,1)S(1)}, bf16[96,2048]{1,0:T(8,128)(2,1)S(1)}, u32[]{:S(2)}, u32[]{:S(2)}) %collective-permute-start.4) | collective-permute-done | bytes 393248 | tf_op jit(solution)/shard_map/ppermute | solution.py:382
  90.1 3.2 %collective-permute-start.19 = (bf16[96,2048]{1,0:T(8,128)(2,1)S(1)}, bf16[96,2048]{1,0:T(8,128)(2,1)S(1)}, u32[]{:S(2)}, u32[]{:S(2)}) collective-permute-start(bf16[96,2048]{1,0:T(8,128)(2,1)S(1)} %get-tuple-element.42), channel_id=1, source_target_pairs={{0,1},{1,0},{2,3},{3,2},{4,5},{5,4},{6,7},{7,6},{8,9},{9,8},{10,11... | collective-permute-start | bytes 1179656 | tf_op jit(solution)/shard_map/ppermute | solution.py:399
  95.6 7.5 %forward.1 = (bf16[512,2048]{1,0:T(8,128)(2,1)S(1)}, bf16[512,1024]{1,0:T(8,128)(2,1)S(1)}, f32[512,1024]{1,0:T(8,128)}) custom-call(bf16[160,2048]{1,0:T(8,128)(2,1)S(1)} %get-tuple-element.37.own1, bf16[96,2048]{1,0:T(8,128)(2,1)S(1)} %get-tuple-element.40.own2, bf16[160,2048]{1,0:T(8,128)(2,1)S(1)} %collective-permute-done.18.got1, ...), custom_call_target="tpu_custom_call" | custom-call | tf_op jit(solution)/shard_map/forward/pallas_call | solution.py:427
  103.1 12.3 %backward.1 = (bf16[512,2048]{1,0:T(8,128)(2,1)S(1)}, bf16[512,1024]{1,0:T(8,128)(2,1)S(1)}, bf16[16,32,2048]{2,1,0:T(8,128)(2,1)}) custom-call(s32[1]{0:T(128)} %bitcast.4.me, bf16[160,2048]{1,0:T(8,128)(2,1)S(1)} %get-tuple-element.31.own1, bf16[96,2048]{1,0:T(8,128)(2,1)S(1)} %get-tuple-element.34.own2, ...), custom_call_target="tpu_custom_call" | custom-call | tf_op jit(solution)/shard_map/backward/pallas_call | solution.py:436
  116.9 9.6 %grads.1 = bf16[2048,2048]{1,0:T(8,128)(2,1)} custom-call(bf16[512,2048]{1,0:T(8,128)(2,1)S(1)} %get-tuple-element.53.inputs, bf16[512,2048]{1,0:T(8,128)(2,1)} %copy-done.2, bf16[512,1024]{1,0:T(8,128)(2,1)S(1)} %get-tuple-element.55.back_pre, bf16[512,1024]{1,0:T(8,128)(2,1)S(1)} %get-tuple-element.56.hidden), custom_call_target="tpu_custom_call" | custom-call | tf_op jit(solution)/shard_map/grads/pallas_call | solution.py:450
  126.6 5.7 %all-to-all-start.1 = ((bf16[16,32,2048]{2,1,0:T(8,128)(2,1)}), bf16[16,32,2048]{2,1,0:T(8,128)(2,1)S(1)}, u32[]{:S(2)}, u32[]{:S(2)}) async-start(bf16[16,32,2048]{2,1,0:T(8,128)(2,1)} %get-tuple-element.44), calls=%async_computation.1 | async-start | bytes 4194304 | tf_op jit(solution)/shard_map/all_to_all | solution.py:446
  141.8 39.3 %all-to-all-done.1 = bf16[16,32,2048]{2,1,0:T(8,128)(2,1)S(1)} async-done(((bf16[16,32,2048]{2,1,0:T(8,128)(2,1)}), bf16[16,32,2048]{2,1,0:T(8,128)(2,1)S(1)}, u32[]{:S(2)}, u32[]{:S(2)}) %all-to-all-start.1) | async-done | bytes 2097184 | tf_op jit(solution)/shard_map/all_to_all | solution.py:446
  183.3 6.9 %all-to-all-start.2 = ((bf16[16,128,128]{2,1,0:T(8,128)(2,1)}), bf16[16,128,128]{2,1,0:T(8,128)(2,1)S(1)}, u32[]{:S(2)}, u32[]{:S(2)}) async-start(bf16[16,128,128]{2,1,0:T(8,128)(2,1)} %undo.1), calls=%async_computation.2 | async-start | bytes 1048576 | tf_op jit(solution)/shard_map/all_to_all | solution.py:468
  190.3 10.3 %all-to-all-done.2.pencil = bf16[16,128,128]{2,1,0:T(8,128)(2,1)S(1)} async-done(((bf16[16,128,128]{2,1,0:T(8,128)(2,1)}), bf16[16,128,128]{2,1,0:T(8,128)(2,1)S(1)}, u32[]{:S(2)}, u32[]{:S(2)}) %all-to-all-start.2) | async-done | bytes 524320 | tf_op jit(solution)/shard_map/all_to_all | solution.py:468
  201.6 3.8 %all-to-all-start.3 = ((bf16[16,128,128]{2,1,0:T(8,128)(2,1)}), bf16[16,128,128]{2,1,0:T(8,128)(2,1)S(1)}, u32[]{:S(2)}, u32[]{:S(2)}) async-start(bf16[16,128,128]{2,1,0:T(8,128)(2,1)} %temporal.1), calls=%async_computation.3 | async-start | bytes 1048576 | tf_op jit(solution)/shard_map/all_to_all | solution.py:472
  205.4 12.5 %all-to-all-done.3.spatial = bf16[16,128,128]{2,1,0:T(8,128)(2,1)S(1)} async-done(((bf16[16,128,128]{2,1,0:T(8,128)(2,1)}), bf16[16,128,128]{2,1,0:T(8,128)(2,1)S(1)}, u32[]{:S(2)}, u32[]{:S(2)}) %all-to-all-start.3) | async-done | bytes 524320 | tf_op jit(solution)/shard_map/all_to_all | solution.py:472
  220.4 2.4 scan.1
  223.7 8.6 %all-to-all-start.4 = ((f32[16,16,128]{2,1,0:T(8,128)}), f32[16,16,128]{2,1,0:T(8,128)S(1)}, u32[]{:S(2)}, u32[]{:S(2)}) async-start(f32[16,16,128]{2,1,0:T(8,128)} %get-tuple-element.49), calls=%async_computation.4 | async-start | bytes 262144 | tf_op jit(solution)/shard_map/all_to_all | solution.py:479
  233.0 8.5 %all-to-all-done.4.heads = f32[16,16,128]{2,1,0:T(8,128)S(1)} async-done(((f32[16,16,128]{2,1,0:T(8,128)}), f32[16,16,128]{2,1,0:T(8,128)S(1)}, u32[]{:S(2)}, u32[]{:S(2)}) %all-to-all-start.4) | async-done | bytes 131104 | tf_op jit(solution)/shard_map/all_to_all | solution.py:479
  (125 shorter events, 45.2 us)
Async XLA Ops:
  7.2 18.3 %collective-permute-start.10 = (bf16[128,2048]{1,0:T(8,128)(2,1)}, bf16[128,2048]{1,0:T(8,128)(2,1)S(1)}, u32[]{:S(2)}, u32[]{:S(2)}) collective-permute-start(bf16[128,2048]{1,0:T(8,128)(2,1)} %bitcast.32), channel_id=1, source_target_pairs={{0,2},{1,3},{2,4},{3,5},{4,6},{5,7},{6,8},{7,9},{8,10},{9,11},{10,... | collective-permute-start | bytes 1572872 | tf_op jit(solution)/shard_map/ppermute | solution.py:364
  9.7 15.8 %collective-permute-start.12 = (bf16[128,2048]{1,0:T(8,128)(2,1)}, bf16[128,2048]{1,0:T(8,128)(2,1)S(1)}, u32[]{:S(2)}, u32[]{:S(2)}) collective-permute-start(bf16[128,2048]{1,0:T(8,128)(2,1)} %bitcast.33), channel_id=1, source_target_pairs={{0,14},{1,15},{2,0},{3,1},{4,2},{5,3},{6,4},{7,5},{8,6},{9,7},{10,... | collective-permute-start | bytes 1572872 | tf_op jit(solution)/shard_map/ppermute | solution.py:364
  13.7 23.1 %collective-permute-start = (bf16[128,2048]{1,0:T(8,128)(2,1)}, bf16[128,2048]{1,0:T(8,128)(2,1)}, u32[]{:S(2)}, u32[]{:S(2)}) collective-permute-start(bf16[128,2048]{1,0:T(8,128)(2,1)} %bitcast.28), channel_id=1, source_target_pairs={{0,2},{1,3},{2,4},{3,5},{4,6},{5,7},{6,8},{7,9},{8,10},{9,11},{10,... | collective-permute-start | bytes 1572872 | tf_op jit(solution)/shard_map/ppermute | solution.py:364
  13.7 23.1 %collective-permute-start.2 = (bf16[128,2048]{1,0:T(8,128)(2,1)}, bf16[128,2048]{1,0:T(8,128)(2,1)}, u32[]{:S(2)}, u32[]{:S(2)}) collective-permute-start(bf16[128,2048]{1,0:T(8,128)(2,1)} %bitcast.29), channel_id=1, source_target_pairs={{0,14},{1,15},{2,0},{3,1},{4,2},{5,3},{6,4},{7,5},{8,6},{9,7},{10,... | collective-permute-start | bytes 1572872 | tf_op jit(solution)/shard_map/ppermute | solution.py:364
  25.5 39.3 %collective-permute-start.11 = (bf16[128,2048]{1,0:T(8,128)(2,1)S(1)}, bf16[128,2048]{1,0:T(8,128)(2,1)S(1)}, u32[]{:S(2)}, u32[]{:S(2)}) collective-permute-start(bf16[128,2048]{1,0:T(8,128)(2,1)S(1)} %collective-permute-done.10.refs_1_), channel_id=1, source_target_pairs={{0,2},{1,3},{2,4},{3,5},{4,6},{5,7},{6,8},{7,9},{8,10},{9,11},{10,... | collective-permute-start | bytes 1572872 | tf_op jit(solution)/shard_map/ppermute | solution.py:375
  25.5 39.3 %collective-permute-start.13 = (bf16[128,2048]{1,0:T(8,128)(2,1)S(1)}, bf16[128,2048]{1,0:T(8,128)(2,1)S(1)}, u32[]{:S(2)}, u32[]{:S(2)}) collective-permute-start(bf16[128,2048]{1,0:T(8,128)(2,1)S(1)} %collective-permute-done.12.refs_3_), channel_id=1, source_target_pairs={{0,14},{1,15},{2,0},{3,1},{4,2},{5,3},{6,4},{7,5},{8,6},{9,7},{10,... | collective-permute-start | bytes 1572872 | tf_op jit(solution)/shard_map/ppermute | solution.py:375
  36.8 31.9 %collective-permute-start.1 = (bf16[128,2048]{1,0:T(8,128)(2,1)}, bf16[128,2048]{1,0:T(8,128)(2,1)S(1)}, u32[]{:S(2)}, u32[]{:S(2)}) collective-permute-start(bf16[128,2048]{1,0:T(8,128)(2,1)} %collective-permute-done.refs_1_), channel_id=1, source_target_pairs={{0,2},{1,3},{2,4},{3,5},{4,6},{5,7},{6,8},{7,9},{8,10},{9,11},{10,... | collective-permute-start | bytes 1572872 | tf_op jit(solution)/shard_map/ppermute | solution.py:375
  36.9 31.9 %collective-permute-start.3 = (bf16[128,2048]{1,0:T(8,128)(2,1)}, bf16[128,2048]{1,0:T(8,128)(2,1)S(1)}, u32[]{:S(2)}, u32[]{:S(2)}) collective-permute-start(bf16[128,2048]{1,0:T(8,128)(2,1)} %collective-permute-done.2.refs_3_), channel_id=1, source_target_pairs={{0,14},{1,15},{2,0},{3,1},{4,2},{5,3},{6,4},{7,5},{8,6},{9,7},{10,... | collective-permute-start | bytes 1572872 | tf_op jit(solution)/shard_map/ppermute | solution.py:375
  42.1 22.7 %all-to-all-start = ((f32[16,24,128]{2,1,0:T(8,128)}), f32[16,24,128]{2,1,0:T(8,128)S(1)}, u32[]{:S(2)}, u32[]{:S(2)}) async-start(f32[16,24,128]{2,1,0:T(8,128)} %info.1), calls=%async_computation | async-start | bytes 393216 | tf_op jit(solution)/shard_map/all_to_all | solution.py:372
  50.6 193.4 %reduce-scatter.2.cloned.1.call-start = ((), (), s32[]{:S(2)}) async-start(), calls=%async_computation.6 | async-start | bytes 8912896 | tf_op jit(solution)/shard_map/reduce_scatter | solution.py:463
  65.5 13.7 %collective-permute-start.14 = (bf16[96,2048]{1,0:T(8,128)(2,1)S(1)}, bf16[96,2048]{1,0:T(8,128)(2,1)S(1)}, u32[]{:S(2)}, u32[]{:S(2)}) collective-permute-start(bf16[96,2048]{1,0:T(8,128)(2,1)S(1)} %get-tuple-element.38), channel_id=1, source_target_pairs={{0,2},{1,3},{2,4},{3,5},{4,6},{5,7},{6,8},{7,9},{8,10},{9,11},{10,... | collective-permute-start | bytes 1179656 | tf_op jit(solution)/shard_map/ppermute | solution.py:382
  68.7 11.1 %collective-permute-start.15 = (bf16[96,2048]{1,0:T(8,128)(2,1)S(1)}, bf16[96,2048]{1,0:T(8,128)(2,1)S(1)}, u32[]{:S(2)}, u32[]{:S(2)}) collective-permute-start(bf16[96,2048]{1,0:T(8,128)(2,1)S(1)} %get-tuple-element.39), channel_id=1, source_target_pairs={{0,14},{1,15},{2,0},{3,1},{4,2},{5,3},{6,4},{7,5},{8,6},{9,7},{10,... | collective-permute-start | bytes 1179656 | tf_op jit(solution)/shard_map/ppermute | solution.py:383
  69.4 16.8 %collective-permute-start.4 = (bf16[96,2048]{1,0:T(8,128)(2,1)S(1)}, bf16[96,2048]{1,0:T(8,128)(2,1)S(1)}, u32[]{:S(2)}, u32[]{:S(2)}) collective-permute-start(bf16[96,2048]{1,0:T(8,128)(2,1)S(1)} %get-tuple-element.32), channel_id=1, source_target_pairs={{0,2},{1,3},{2,4},{3,5},{4,6},{5,7},{6,8},{7,9},{8,10},{9,11},{10,... | collective-permute-start | bytes 1179656 | tf_op jit(solution)/shard_map/ppermute | solution.py:382
  70.9 16.3 %collective-permute-start.5 = (bf16[96,2048]{1,0:T(8,128)(2,1)S(1)}, bf16[96,2048]{1,0:T(8,128)(2,1)S(1)}, u32[]{:S(2)}, u32[]{:S(2)}) collective-permute-start(bf16[96,2048]{1,0:T(8,128)(2,1)S(1)} %get-tuple-element.33), channel_id=1, source_target_pairs={{0,14},{1,15},{2,0},{3,1},{4,2},{5,3},{6,4},{7,5},{8,6},{9,7},{10,... | collective-permute-start | bytes 1179656 | tf_op jit(solution)/shard_map/ppermute | solution.py:383
  75.4 20.2 %collective-permute-start.18 = (bf16[160,2048]{1,0:T(8,128)(2,1)S(1)}, bf16[160,2048]{1,0:T(8,128)(2,1)S(1)}, u32[]{:S(2)}, u32[]{:S(2)}) collective-permute-start(bf16[160,2048]{1,0:T(8,128)(2,1)S(1)} %get-tuple-element.41), channel_id=1, source_target_pairs={{0,1},{1,0},{2,3},{3,2},{4,5},{5,4},{6,7},{7,6},{8,9},{9,8},{10,11... | collective-permute-start | bytes 1966088 | tf_op jit(solution)/shard_map/ppermute | solution.py:392
  79.2 9.8 %collective-permute-start.16 = (bf16[32,2048]{1,0:T(8,128)(2,1)S(1)}, bf16[32,2048]{1,0:T(8,128)(2,1)S(1)}, u32[]{:S(2)}, u32[]{:S(2)}) collective-permute-start(bf16[32,2048]{1,0:T(8,128)(2,1)S(1)} %slice.86), channel_id=1, source_target_pairs={{0,2},{1,3},{2,4},{3,5},{4,6},{5,7},{6,8},{7,9},{8,10},{9,11},{10,... | collective-permute-start | bytes 393224 | tf_op jit(solution)/shard_map/ppermute | solution.py:384
  79.9 23.3 %collective-permute-start.8 = (bf16[160,2048]{1,0:T(8,128)(2,1)S(1)}, bf16[160,2048]{1,0:T(8,128)(2,1)S(1)}, u32[]{:S(2)}, u32[]{:S(2)}) collective-permute-start(bf16[160,2048]{1,0:T(8,128)(2,1)S(1)} %get-tuple-element.35), channel_id=1, source_target_pairs={{0,1},{1,0},{2,3},{3,2},{4,5},{5,4},{6,7},{7,6},{8,9},{9,8},{10,11... | collective-permute-start | bytes 1966088 | tf_op jit(solution)/shard_map/ppermute | solution.py:392
  87.3 6.0 %collective-permute-start.6 = (bf16[32,2048]{1,0:T(8,128)(2,1)S(1)}, bf16[32,2048]{1,0:T(8,128)(2,1)S(1)}, u32[]{:S(2)}, u32[]{:S(2)}) collective-permute-start(bf16[32,2048]{1,0:T(8,128)(2,1)S(1)} %slice.84), channel_id=1, source_target_pairs={{0,2},{1,3},{2,4},{3,5},{4,6},{5,7},{6,8},{7,9},{8,10},{9,11},{10,... | collective-permute-start | bytes 393224 | tf_op jit(solution)/shard_map/ppermute | solution.py:384
  90.1 5.5 %collective-permute-start.19 = (bf16[96,2048]{1,0:T(8,128)(2,1)S(1)}, bf16[96,2048]{1,0:T(8,128)(2,1)S(1)}, u32[]{:S(2)}, u32[]{:S(2)}) collective-permute-start(bf16[96,2048]{1,0:T(8,128)(2,1)S(1)} %get-tuple-element.42), channel_id=1, source_target_pairs={{0,1},{1,0},{2,3},{3,2},{4,5},{5,4},{6,7},{7,6},{8,9},{9,8},{10,11... | collective-permute-start | bytes 1179656 | tf_op jit(solution)/shard_map/ppermute | solution.py:399
  93.8 9.3 %collective-permute-start.9 = (bf16[96,2048]{1,0:T(8,128)(2,1)S(1)}, bf16[96,2048]{1,0:T(8,128)(2,1)S(1)}, u32[]{:S(2)}, u32[]{:S(2)}) collective-permute-start(bf16[96,2048]{1,0:T(8,128)(2,1)S(1)} %get-tuple-element.36), channel_id=1, source_target_pairs={{0,1},{1,0},{2,3},{3,2},{4,5},{5,4},{6,7},{7,6},{8,9},{9,8},{10,11... | collective-permute-start | bytes 1179656 | tf_op jit(solution)/shard_map/ppermute | solution.py:399
  126.6 54.6 %all-to-all-start.1 = ((bf16[16,32,2048]{2,1,0:T(8,128)(2,1)}), bf16[16,32,2048]{2,1,0:T(8,128)(2,1)S(1)}, u32[]{:S(2)}, u32[]{:S(2)}) async-start(bf16[16,32,2048]{2,1,0:T(8,128)(2,1)} %get-tuple-element.44), calls=%async_computation.1 | async-start | bytes 4194304 | tf_op jit(solution)/shard_map/all_to_all | solution.py:446
  183.3 17.3 %all-to-all-start.2 = ((bf16[16,128,128]{2,1,0:T(8,128)(2,1)}), bf16[16,128,128]{2,1,0:T(8,128)(2,1)S(1)}, u32[]{:S(2)}, u32[]{:S(2)}) async-start(bf16[16,128,128]{2,1,0:T(8,128)(2,1)} %undo.1), calls=%async_computation.2 | async-start | bytes 1048576 | tf_op jit(solution)/shard_map/all_to_all | solution.py:468
  201.6 16.3 %all-to-all-start.3 = ((bf16[16,128,128]{2,1,0:T(8,128)(2,1)}), bf16[16,128,128]{2,1,0:T(8,128)(2,1)S(1)}, u32[]{:S(2)}, u32[]{:S(2)}) async-start(bf16[16,128,128]{2,1,0:T(8,128)(2,1)} %temporal.1), calls=%async_computation.3 | async-start | bytes 1048576 | tf_op jit(solution)/shard_map/all_to_all | solution.py:472
  223.7 17.8 %all-to-all-start.4 = ((f32[16,16,128]{2,1,0:T(8,128)}), f32[16,16,128]{2,1,0:T(8,128)S(1)}, u32[]{:S(2)}, u32[]{:S(2)}) async-start(f32[16,16,128]{2,1,0:T(8,128)} %get-tuple-element.49), calls=%async_computation.4 | async-start | bytes 262144 | tf_op jit(solution)/shard_map/all_to_all | solution.py:479
  (28 other events, 223.2 us)
Sparse Core Ops, SparseCore 0:
  126.6 93.2 reduce-scatter.1

commit v2 on v1

--- a/solution.py
+++ b/solution.py
@@ -11,7 +11,7 @@
 TOPK = 2
 LANES = 128
 SUB = 8
-VMEM_LIMIT = 48 * 1024 * 1024
+VMEM_LIMIT = 20 * 1024 * 1024
 
 GELU_SCALE = 0.7978845608028654
 GELU_CUBIC = 0.044715
@@ -47,17 +47,13 @@
     )
 
 
-def info_kernel(facts, rate, info, head):
-    experts = info.shape[0]
+def info_kernel(facts, rate, info):
     blocks = rate.shape[1] // LANES
     total = jnp.exp(-jnp.sum(rate[...].astype(jnp.float32), axis=0, keepdims=True))
     for b in range(blocks):
-        head[b : b + 1, :] = total[:, b * LANES : (b + 1) * LANES]
-    spread = head[...]
-    for e in range(experts):
-        info[e, 0:blocks, :] = spread
-        info[e, blocks : blocks + 4, :] = facts[...]
-        info[e, blocks + 4 : blocks + 8, :] = jnp.zeros((4, LANES), jnp.float32)
+        info[b : b + 1, :] = total[:, b * LANES : (b + 1) * LANES]
+    info[blocks : blocks + 4, :] = facts[...]
+    info[blocks + 4 : blocks + 8, :] = jnp.zeros((4, LANES), jnp.float32)
 
 
 def chosen_rows(info, source, experts, x, gated, put):
@@ -168,14 +164,15 @@
     step = 256
 
     def part(n, _):
-        at = pl.ds(pl.multiple_of(n * step, step), step)
+        at = pl.ds(n * step, step)
         pre = jnp.dot(inputs[...], weight_in[:, at], preferred_element_type=jnp.float32)
         value, rise = gelu_parts(pre)
         hidden[:, at] = value.astype(jnp.bfloat16)
         slope[:, at] = rise
         return 0
 
-    lax.fori_loop(0, hidden.shape[1] // step, part, 0)
+    for n in range(hidden.shape[1] // step):
+        part(n, 0)
 
 
 def backward_kernel(
@@ -185,12 +182,13 @@
     step = 256
 
     def part(n, _):
-        at = pl.ds(pl.multiple_of(n * step, step), step)
+        at = pl.ds(n * step, step)
         back_hidden = jnp.dot(routed[...], weight_out[:, at], preferred_element_type=jnp.float32)
         back_pre[:, at] = (back_hidden * slope[:, at]).astype(jnp.bfloat16)
         return 0
 
-    lax.fori_loop(0, back_pre.shape[1] // step, part, 0)
+    for n in range(back_pre.shape[1] // step):
+        part(n, 0)
     e = me[0]
     z, core = e // 2, e % 2
     targets = []
@@ -198,7 +196,7 @@
         targets += [2 * ((z + away + 8) % 8) + owner for away in NEAR + FAR]
 
     def route(n, _):
-        at = pl.ds(pl.multiple_of(n * step, step), step)
+        at = pl.ds(n * step, step)
         rows = lax.dot_general(
             back_pre[...],
             weight_in[at, :],
@@ -209,10 +207,11 @@
             back[target, :, at] = rows[32 * i : 32 * i + 32]
         return 0
 
-    lax.fori_loop(0, weight_in.shape[0] // step, route, 0)
-
-
-def grads_kernel(scale, inputs, routed, back_pre, hidden, out):
+    for n in range(weight_in.shape[0] // step):
+        route(n, 0)
+
+
+def grads_kernel(scale, inputs, routed, back_pre, hidden, started, out):
     half = back_pre.shape[1]
     out[:, 0:half] = (column_product(inputs[...], back_pre[...]) * scale).astype(jnp.bfloat16)
     out[:, half : 2 * half] = (column_product(routed[...], hidden[...]) * scale).astype(
@@ -363,13 +362,8 @@
     for x in (saved[0], upstream[0]):
         up1, down1 = lax.ppermute(x, "expert", up), lax.ppermute(x, "expert", down)
         chains.append([x, up1, down1])
-    info = call(
-        info_kernel,
-        shape((experts, blocks + 8, LANES), f32),
-        "info",
-        scratch_shapes=[pltpu.VMEM((blocks, LANES), f32)],
-    )(facts, rate)
-    got_info = lax.all_to_all(info, "expert", split_axis=0, concat_axis=0, tiled=True)
+    info = call(info_kernel, shape((blocks + 8, LANES), f32), "info")(facts, rate)
+    got_info = lax.all_gather(info, "expert", axis=0, tiled=False)
     pieces = []
     for gated, (x, up1, down1) in enumerate(chains):
         up2, down2 = lax.ppermute(up1, "expert", up), lax.ppermute(down1, "expert", down)
@@ -446,7 +440,8 @@
     returned = lax.all_to_all(
         back_slots, "expert", split_axis=0, concat_axis=0, tiled=True
     ).reshape(slots, width)
-    step = 256
+    started = lax.ppermute(back_slots[0, :16, :LANES], "expert", swap)
+    step = 512
     partial = call(
         functools.partial(grads_kernel, scale),
         shape((width, 2 * hidden_width), bf16),
@@ -457,9 +452,10 @@
             pl.BlockSpec((slots, step), lambda i: (0, i)),
             pl.BlockSpec((slots, hidden_width), lambda i: (0, 0)),
             pl.BlockSpec((slots, hidden_width), lambda i: (0, 0)),
+            pl.BlockSpec(memory_space=pl.ANY),
         ],
         out_specs=pl.BlockSpec((step, 2 * hidden_width), lambda i: (i, 0)),
-    )(inputs_all, routed_all, back_pre, hidden)
+    )(inputs_all, routed_all, back_pre, hidden, started)
     weight_rows = lax.psum_scatter(partial, "frame", scatter_dimension=0, tiled=True)
     grad_in = weight_rows[:, :hidden_width][None]
     grad_out = weight_rows[:, hidden_width:][None]

time: 254 us -> 250 us (0.984)
  blocking collectives: 0 us -> 30.7 us
  Pallas kernels: 43.1 us -> 24.1 us
  starting transfers between devices: 64.3 us -> 54.9 us
  waiting for transfers between devices: 109 us -> 101 us
    all_gather x0 -> x1, blocking collectives: none -> 30.7 us  [body(): got_info = lax.all_gather(info, 'expert', axis=0, tiled=False)]
    all_to_all x1 -> x0, waiting for transfers between devices: 14.1 us -> none  [body(): lax.all_to_all(info, 'expert', split_axis=0, concat_axis=0, tiled=True)]
    all_to_all x1 -> x0, starting transfers between devices: 8.54 us -> none  [body(): lax.all_to_all(info, 'expert', split_axis=0, concat_axis=0, tiled=True)]
    all_to_all x1, waiting for transfers between devices: 39.3 us -> 47.3 us  [body(): lax.all_to_all(back_slots, 'expert', split_axis=0, concat_axis=0, tiled=T...]
    pallas_call x1, Pallas kernels: 12.3 us -> 4.71 us  [body(): call(backward_kernel, (shape((slots, width), bf16), shape((slots, hidden_...]
    all_to_all x1, waiting for transfers between devices: 12.5 us -> 7.16 us  [body(): lax.all_to_all(pencil, 'frame', split_axis=0, concat_axis=0, tiled=True)]
    ppermute x2, starting transfers between devices: 4.81 us -> 0.17 us  [body(): up3 = lax.ppermute(packed[0], 'expert', up)]
    ppermute x2, starting transfers between devices: 1.22 us -> 5.32 us  [body(): down3 = lax.ppermute(packed[1], 'expert', down)]
  transfers between devices with their start and end apart: 26 -> 26, of which waited for: 11 -> 12; matrix products, arithmetic and copies ran while one was open for 1% -> 1% of each run, Pallas kernels for 8% -> 6%
where the time goes in v2:
time: 250 us; the launch traced here: 249 us
  waiting for transfers between devices  101 us (40%)
  starting transfers between devices  54.9 us (22%)
  blocking collectives  30.7 us (12%)
  Pallas kernels  24.1 us (10%)
  local copies, waits for them, and re-layouts  21 us (8%)
  between operations  14.5 us (6%)
  other arithmetic  2.8 us (1%)
    all_to_all x1, waiting for transfers between devices, body(): lax.all_to_all(back_slots, 'expert', split_axis=0, concat_axis=0, tiled=T...  47.3 us
    all_gather x1, blocking collectives, body(): got_info = lax.all_gather(info, 'expert', axis=0, tiled=False)  30.7 us
    unnamed x63, local copies, waits for them, and re-layouts  18.9 us
    ppermute x2, waiting for transfers between devices, body(): lax.ppermute(x, 'expert', up)  16.9 us
    all_to_all x1, waiting for transfers between devices, body(): lax.all_to_all(mixed, 'frame', split_axis=0, concat_axis=0, tiled=True)  9.6 us
    all_to_all x1, waiting for transfers between devices, body(): lax.all_to_all(heads, 'expert', split_axis=0, concat_axis=0, tiled=True)  8.55 us
    all_to_all x1, starting transfers between devices, body(): lax.all_to_all(heads, 'expert', split_axis=0, concat_axis=0, tiled=True)  8.42 us
    ppermute x2, waiting for transfers between devices, body(): up3 = lax.ppermute(packed[0], 'expert', up)  7.37 us
  transfers between devices with their start and end apart: 26, of which 12 were waited for; matrix products, arithmetic and copies ran while one was open for 1% of the time, Pallas kernels for 6%

profile of v2, /device:TPU:1, one launch (start us, length us, event | category | flops | bytes accessed | tf_op | source)
XLA Modules:
  0.0 248.9 jit_solution(5475220989101669202)
XLA Ops:
  7.2 2.5 %collective-permute-start.10 = (bf16[128,2048]{1,0:T(8,128)(2,1)}, bf16[128,2048]{1,0:T(8,128)(2,1)S(1)}, u32[]{:S(2)}, u32[]{:S(2)}) collective-permute-start(bf16[128,2048]{1,0:T(8,128)(2,1)} %bitcast.50), channel_id=1, source_target_pairs={{0,2},{1,3},{2,4},{3,5},{4,6},{5,7},{6,8},{7,9},{8,10},{9,11},{10,... | collective-permute-start | bytes 1572872 | tf_op jit(solution)/shard_map/ppermute | solution.py:363
  9.8 4.0 %collective-permute-start.12 = (bf16[128,2048]{1,0:T(8,128)(2,1)}, bf16[128,2048]{1,0:T(8,128)(2,1)S(1)}, u32[]{:S(2)}, u32[]{:S(2)}) collective-permute-start(bf16[128,2048]{1,0:T(8,128)(2,1)} %bitcast.51), channel_id=1, source_target_pairs={{0,14},{1,15},{2,0},{3,1},{4,2},{5,3},{6,4},{7,5},{8,6},{9,7},{10,... | collective-permute-start | bytes 1572872 | tf_op jit(solution)/shard_map/ppermute | solution.py:363
  13.8 2.7 %collective-permute-start.2 = (bf16[128,2048]{1,0:T(8,128)(2,1)}, bf16[128,2048]{1,0:T(8,128)(2,1)S(1)}, u32[]{:S(2)}, u32[]{:S(2)}) collective-permute-start(bf16[128,2048]{1,0:T(8,128)(2,1)} %bitcast.47), channel_id=1, source_target_pairs={{0,14},{1,15},{2,0},{3,1},{4,2},{5,3},{6,4},{7,5},{8,6},{9,7},{10,... | collective-permute-start | bytes 1572872 | tf_op jit(solution)/shard_map/ppermute | solution.py:363
  16.5 9.1 %collective-permute-done.10.refs_1_ = bf16[128,2048]{1,0:T(8,128)(2,1)S(1)} collective-permute-done((bf16[128,2048]{1,0:T(8,128)(2,1)}, bf16[128,2048]{1,0:T(8,128)(2,1)S(1)}, u32[]{:S(2)}, u32[]{:S(2)}) %collective-permute-start.10) | collective-permute-done | bytes 524320 | tf_op jit(solution)/shard_map/ppermute | solution.py:363
  25.6 2.7 %collective-permute-start.13 = (bf16[128,2048]{1,0:T(8,128)(2,1)S(1)}, bf16[128,2048]{1,0:T(8,128)(2,1)S(1)}, u32[]{:S(2)}, u32[]{:S(2)}) collective-permute-start(bf16[128,2048]{1,0:T(8,128)(2,1)S(1)} %collective-permute-done.12.refs_3_), channel_id=1, source_target_pairs={{0,14},{1,15},{2,0},{3,1},{4,2},{5,3},{6,4},{7,5},{8,6},{9,7},{10,... | collective-permute-start | bytes 1572872 | tf_op jit(solution)/shard_map/ppermute | solution.py:369
  29.0 7.8 %collective-permute-done.refs_1_ = bf16[128,2048]{1,0:T(8,128)(2,1)S(1)} collective-permute-done((bf16[128,2048]{1,0:T(8,128)(2,1)}, bf16[128,2048]{1,0:T(8,128)(2,1)S(1)}, u32[]{:S(2)}, u32[]{:S(2)}) %collective-permute-start) | collective-permute-done | bytes 524320 | tf_op jit(solution)/shard_map/ppermute | solution.py:363
  36.8 2.7 %collective-permute-start.3 = (bf16[128,2048]{1,0:T(8,128)(2,1)S(1)}, bf16[128,2048]{1,0:T(8,128)(2,1)S(1)}, u32[]{:S(2)}, u32[]{:S(2)}) collective-permute-start(bf16[128,2048]{1,0:T(8,128)(2,1)S(1)} %collective-permute-done.2.refs_3_), channel_id=1, source_target_pairs={{0,14},{1,15},{2,0},{3,1},{4,2},{5,3},{6,4},{7,5},{8,6},{9,7},{10,... | collective-permute-start | bytes 1572872 | tf_op jit(solution)/shard_map/ppermute | solution.py:369
  42.0 30.7 %all-gather = f32[384,128]{1,0:T(8,128)S(1)} all-gather(f32[24,128]{1,0:T(8,128)S(1)} %info.1), channel_id=2, replica_groups=mesh['frame'=16,'expert'=16] {'expert'}, dimensions={0}, use_global_device_ids=true | all-gather | bytes 208896 | tf_op jit(solution)/shard_map/all_gather | solution.py:366
  73.5 2.7 %collective-permute-start.15 = (bf16[96,2048]{1,0:T(8,128)(2,1)S(1)}, bf16[96,2048]{1,0:T(8,128)(2,1)S(1)}, u32[]{:S(2)}, u32[]{:S(2)}) collective-permute-start(bf16[96,2048]{1,0:T(8,128)(2,1)S(1)} %get-tuple-element.39), channel_id=1, source_target_pairs={{0,14},{1,15},{2,0},{3,1},{4,2},{5,3},{6,4},{7,5},{8,6},{9,7},{10,... | collective-permute-start | bytes 1179656 | tf_op jit(solution)/shard_map/ppermute | solution.py:377
  76.9 2.7 %collective-permute-start.5 = (bf16[96,2048]{1,0:T(8,128)(2,1)S(1)}, bf16[96,2048]{1,0:T(8,128)(2,1)S(1)}, u32[]{:S(2)}, u32[]{:S(2)}) collective-permute-start(bf16[96,2048]{1,0:T(8,128)(2,1)S(1)} %get-tuple-element.33), channel_id=1, source_target_pairs={{0,14},{1,15},{2,0},{3,1},{4,2},{5,3},{6,4},{7,5},{8,6},{9,7},{10,... | collective-permute-start | bytes 1179656 | tf_op jit(solution)/shard_map/ppermute | solution.py:377
  87.0 6.7 %collective-permute-done.4.up3 = bf16[96,2048]{1,0:T(8,128)(2,1)S(1)} collective-permute-done((bf16[96,2048]{1,0:T(8,128)(2,1)S(1)}, bf16[96,2048]{1,0:T(8,128)(2,1)S(1)}, u32[]{:S(2)}, u32[]{:S(2)}) %collective-permute-start.4) | collective-permute-done | bytes 393248 | tf_op jit(solution)/shard_map/ppermute | solution.py:376
  97.5 3.4 %collective-permute-start.19 = (bf16[96,2048]{1,0:T(8,128)(2,1)S(1)}, bf16[96,2048]{1,0:T(8,128)(2,1)S(1)}, u32[]{:S(2)}, u32[]{:S(2)}) collective-permute-start(bf16[96,2048]{1,0:T(8,128)(2,1)S(1)} %get-tuple-element.42), channel_id=1, source_target_pairs={{0,1},{1,0},{2,3},{3,2},{4,5},{5,4},{6,7},{7,6},{8,9},{9,8},{10,11... | collective-permute-start | bytes 1179656 | tf_op jit(solution)/shard_map/ppermute | solution.py:393
  103.1 3.5 %forward.1 = (bf16[512,2048]{1,0:T(8,128)(2,1)S(1)}, bf16[512,1024]{1,0:T(8,128)(2,1)S(1)}, f32[512,1024]{1,0:T(8,128)S(1)}) custom-call(bf16[160,2048]{1,0:T(8,128)(2,1)S(1)} %get-tuple-element.37.own1, bf16[96,2048]{1,0:T(8,128)(2,1)S(1)} %get-tuple-element.40.own2, bf16[160,2048]{1,0:T(8,128)(2,1)S(1)} %collective-permute-done.18.got1, ...), custom_call_target="tpu_custom_call" | custom-call | tf_op jit(solution)/shard_map/forward/pallas_call | solution.py:421
  106.6 4.7 %backward.1 = (bf16[512,2048]{1,0:T(8,128)(2,1)S(1)}, bf16[512,1024]{1,0:T(8,128)(2,1)S(1)}, bf16[16,32,2048]{2,1,0:T(8,128)(2,1)S(1)}) custom-call(s32[1]{0:T(128)} %bitcast.4.me, bf16[160,2048]{1,0:T(8,128)(2,1)S(1)} %get-tuple-element.31.own1, bf16[96,2048]{1,0:T(8,128)(2,1)S(1)} %get-tuple-element.34.own2, ...), custom_call_target="tpu_custom_call" | custom-call | tf_op jit(solution)/shard_map/backward/pallas_call | solution.py:430
  112.8 5.5 %grads.1 = bf16[2048,2048]{1,0:T(8,128)(2,1)S(1)} custom-call(bf16[512,2048]{1,0:T(8,128)(2,1)S(1)} %get-tuple-element.53.inputs, bf16[512,2048]{1,0:T(8,128)(2,1)S(1)} %get-tuple-element.54.routed, bf16[512,1024]{1,0:T(8,128)(2,1)S(1)} %get-tuple-element.55.back_pre, bf16[512,1024]{1,0:T(8,128)(2,1)S(1)} %get-tuple-element.56.hidden, ...), custom_call_target="tpu_custom_call" | custom-call | tf_op jit(solution)/shard_map/grads/pallas_call | solution.py:445
  118.4 3.3 %copy-done = bf16[2048,2048]{1,0:T(8,128)(2,1)} copy-done((bf16[2048,2048]{1,0:T(8,128)(2,1)}, bf16[2048,2048]{1,0:T(8,128)(2,1)S(1)}, u32[]{:S(2)}) %copy-start) | copy-done | bytes 8388632
  121.8 5.7 %all-to-all-start = ((bf16[16,32,2048]{2,1,0:T(8,128)(2,1)}), bf16[16,32,2048]{2,1,0:T(8,128)(2,1)S(1)}, u32[]{:S(2)}, u32[]{:S(2)}) async-start(bf16[16,32,2048]{2,1,0:T(8,128)(2,1)} %copy-done.5), calls=%async_computation | async-start | bytes 4194304 | tf_op jit(solution)/shard_map/all_to_all | solution.py:440
  129.1 47.3 %all-to-all-done = bf16[16,32,2048]{2,1,0:T(8,128)(2,1)S(1)} async-done(((bf16[16,32,2048]{2,1,0:T(8,128)(2,1)}), bf16[16,32,2048]{2,1,0:T(8,128)(2,1)S(1)}, u32[]{:S(2)}, u32[]{:S(2)}) %all-to-all-start) | async-done | bytes 2097184 | tf_op jit(solution)/shard_map/all_to_all | solution.py:440
  178.5 6.9 %all-to-all-start.1 = ((bf16[16,128,128]{2,1,0:T(8,128)(2,1)}), bf16[16,128,128]{2,1,0:T(8,128)(2,1)S(1)}, u32[]{:S(2)}, u32[]{:S(2)}) async-start(bf16[16,128,128]{2,1,0:T(8,128)(2,1)} %undo.1), calls=%async_computation.1 | async-start | bytes 1048576 | tf_op jit(solution)/shard_map/all_to_all | solution.py:464
  186.2 9.6 %all-to-all-done.1.pencil = bf16[16,128,128]{2,1,0:T(8,128)(2,1)S(1)} async-done(((bf16[16,128,128]{2,1,0:T(8,128)(2,1)}), bf16[16,128,128]{2,1,0:T(8,128)(2,1)S(1)}, u32[]{:S(2)}, u32[]{:S(2)}) %all-to-all-start.1) | async-done | bytes 524320 | tf_op jit(solution)/shard_map/all_to_all | solution.py:464
  196.7 3.8 %all-to-all-start.2 = ((bf16[16,128,128]{2,1,0:T(8,128)(2,1)}), bf16[16,128,128]{2,1,0:T(8,128)(2,1)S(1)}, u32[]{:S(2)}, u32[]{:S(2)}) async-start(bf16[16,128,128]{2,1,0:T(8,128)(2,1)} %temporal.1), calls=%async_computation.2 | async-start | bytes 1048576 | tf_op jit(solution)/shard_map/all_to_all | solution.py:468
  205.9 7.2 %all-to-all-done.2.spatial = bf16[16,128,128]{2,1,0:T(8,128)(2,1)S(1)} async-done(((bf16[16,128,128]{2,1,0:T(8,128)(2,1)}), bf16[16,128,128]{2,1,0:T(8,128)(2,1)S(1)}, u32[]{:S(2)}, u32[]{:S(2)}) %all-to-all-start.2) | async-done | bytes 524320 | tf_op jit(solution)/shard_map/all_to_all | solution.py:468
  220.1 8.4 %all-to-all-start.3 = ((f32[16,16,128]{2,1,0:T(8,128)}), f32[16,16,128]{2,1,0:T(8,128)S(1)}, u32[]{:S(2)}, u32[]{:S(2)}) async-start(f32[16,16,128]{2,1,0:T(8,128)} %get-tuple-element.49), calls=%async_computation.3 | async-start | bytes 262144 | tf_op jit(solution)/shard_map/all_to_all | solution.py:475
  229.2 8.5 %all-to-all-done.3.heads = f32[16,16,128]{2,1,0:T(8,128)S(1)} async-done(((f32[16,16,128]{2,1,0:T(8,128)}), f32[16,16,128]{2,1,0:T(8,128)S(1)}, u32[]{:S(2)}, u32[]{:S(2)}) %all-to-all-start.3) | async-done | bytes 131104 | tf_op jit(solution)/shard_map/all_to_all | solution.py:475
  (131 shorter events, 42.5 us)
Async XLA Ops:
  7.2 233.1 %reduce-scatter.2.cloned.1.call-start = ((), (), s32[]{:S(2)}) async-start(), calls=%async_computation.5 | async-start | bytes 8912896 | tf_op jit(solution)/shard_map/reduce_scatter | solution.py:459
  7.2 18.3 %collective-permute-start.10 = (bf16[128,2048]{1,0:T(8,128)(2,1)}, bf16[128,2048]{1,0:T(8,128)(2,1)S(1)}, u32[]{:S(2)}, u32[]{:S(2)}) collective-permute-start(bf16[128,2048]{1,0:T(8,128)(2,1)} %bitcast.50), channel_id=1, source_target_pairs={{0,2},{1,3},{2,4},{3,5},{4,6},{5,7},{6,8},{7,9},{8,10},{9,11},{10,... | collective-permute-start | bytes 1572872 | tf_op jit(solution)/shard_map/ppermute | solution.py:363
  9.8 15.8 %collective-permute-start.12 = (bf16[128,2048]{1,0:T(8,128)(2,1)}, bf16[128,2048]{1,0:T(8,128)(2,1)S(1)}, u32[]{:S(2)}, u32[]{:S(2)}) collective-permute-start(bf16[128,2048]{1,0:T(8,128)(2,1)} %bitcast.51), channel_id=1, source_target_pairs={{0,14},{1,15},{2,0},{3,1},{4,2},{5,3},{6,4},{7,5},{8,6},{9,7},{10,... | collective-permute-start | bytes 1572872 | tf_op jit(solution)/shard_map/ppermute | solution.py:363
  13.8 23.0 %collective-permute-start = (bf16[128,2048]{1,0:T(8,128)(2,1)}, bf16[128,2048]{1,0:T(8,128)(2,1)S(1)}, u32[]{:S(2)}, u32[]{:S(2)}) collective-permute-start(bf16[128,2048]{1,0:T(8,128)(2,1)} %bitcast.46), channel_id=1, source_target_pairs={{0,2},{1,3},{2,4},{3,5},{4,6},{5,7},{6,8},{7,9},{8,10},{9,11},{10,... | collective-permute-start | bytes 1572872 | tf_op jit(solution)/shard_map/ppermute | solution.py:363
  13.8 23.0 %collective-permute-start.2 = (bf16[128,2048]{1,0:T(8,128)(2,1)}, bf16[128,2048]{1,0:T(8,128)(2,1)S(1)}, u32[]{:S(2)}, u32[]{:S(2)}) collective-permute-start(bf16[128,2048]{1,0:T(8,128)(2,1)} %bitcast.47), channel_id=1, source_target_pairs={{0,14},{1,15},{2,0},{3,1},{4,2},{5,3},{6,4},{7,5},{8,6},{9,7},{10,... | collective-permute-start | bytes 1572872 | tf_op jit(solution)/shard_map/ppermute | solution.py:363
  25.6 47.2 %collective-permute-start.11 = (bf16[128,2048]{1,0:T(8,128)(2,1)S(1)}, bf16[128,2048]{1,0:T(8,128)(2,1)S(1)}, u32[]{:S(2)}, u32[]{:S(2)}) collective-permute-start(bf16[128,2048]{1,0:T(8,128)(2,1)S(1)} %collective-permute-done.10.refs_1_), channel_id=1, source_target_pairs={{0,2},{1,3},{2,4},{3,5},{4,6},{5,7},{6,8},{7,9},{8,10},{9,11},{10,... | collective-permute-start | bytes 1572872 | tf_op jit(solution)/shard_map/ppermute | solution.py:369
  25.6 47.2 %collective-permute-start.13 = (bf16[128,2048]{1,0:T(8,128)(2,1)S(1)}, bf16[128,2048]{1,0:T(8,128)(2,1)S(1)}, u32[]{:S(2)}, u32[]{:S(2)}) collective-permute-start(bf16[128,2048]{1,0:T(8,128)(2,1)S(1)} %collective-permute-done.12.refs_3_), channel_id=1, source_target_pairs={{0,14},{1,15},{2,0},{3,1},{4,2},{5,3},{6,4},{7,5},{8,6},{9,7},{10,... | collective-permute-start | bytes 1572872 | tf_op jit(solution)/shard_map/ppermute | solution.py:369
  36.8 39.3 %collective-permute-start.1 = (bf16[128,2048]{1,0:T(8,128)(2,1)S(1)}, bf16[128,2048]{1,0:T(8,128)(2,1)S(1)}, u32[]{:S(2)}, u32[]{:S(2)}) collective-permute-start(bf16[128,2048]{1,0:T(8,128)(2,1)S(1)} %collective-permute-done.refs_1_), channel_id=1, source_target_pairs={{0,2},{1,3},{2,4},{3,5},{4,6},{5,7},{6,8},{7,9},{8,10},{9,11},{10,... | collective-permute-start | bytes 1572872 | tf_op jit(solution)/shard_map/ppermute | solution.py:369
  36.8 39.3 %collective-permute-start.3 = (bf16[128,2048]{1,0:T(8,128)(2,1)S(1)}, bf16[128,2048]{1,0:T(8,128)(2,1)S(1)}, u32[]{:S(2)}, u32[]{:S(2)}) collective-permute-start(bf16[128,2048]{1,0:T(8,128)(2,1)S(1)} %collective-permute-done.2.refs_3_), channel_id=1, source_target_pairs={{0,14},{1,15},{2,0},{3,1},{4,2},{5,3},{6,4},{7,5},{8,6},{9,7},{10,... | collective-permute-start | bytes 1572872 | tf_op jit(solution)/shard_map/ppermute | solution.py:369
  73.4 11.8 %collective-permute-start.14 = (bf16[96,2048]{1,0:T(8,128)(2,1)S(1)}, bf16[96,2048]{1,0:T(8,128)(2,1)S(1)}, u32[]{:S(2)}, u32[]{:S(2)}) collective-permute-start(bf16[96,2048]{1,0:T(8,128)(2,1)S(1)} %get-tuple-element.38), channel_id=1, source_target_pairs={{0,2},{1,3},{2,4},{3,5},{4,6},{5,7},{6,8},{7,9},{8,10},{9,11},{10,... | collective-permute-start | bytes 1179656 | tf_op jit(solution)/shard_map/ppermute | solution.py:376
  73.5 11.9 %collective-permute-start.15 = (bf16[96,2048]{1,0:T(8,128)(2,1)S(1)}, bf16[96,2048]{1,0:T(8,128)(2,1)S(1)}, u32[]{:S(2)}, u32[]{:S(2)}) collective-permute-start(bf16[96,2048]{1,0:T(8,128)(2,1)S(1)} %get-tuple-element.39), channel_id=1, source_target_pairs={{0,14},{1,15},{2,0},{3,1},{4,2},{5,3},{6,4},{7,5},{8,6},{9,7},{10,... | collective-permute-start | bytes 1179656 | tf_op jit(solution)/shard_map/ppermute | solution.py:377
  76.8 16.9 %collective-permute-start.4 = (bf16[96,2048]{1,0:T(8,128)(2,1)S(1)}, bf16[96,2048]{1,0:T(8,128)(2,1)S(1)}, u32[]{:S(2)}, u32[]{:S(2)}) collective-permute-start(bf16[96,2048]{1,0:T(8,128)(2,1)S(1)} %get-tuple-element.32), channel_id=1, source_target_pairs={{0,2},{1,3},{2,4},{3,5},{4,6},{5,7},{6,8},{7,9},{8,10},{9,11},{10,... | collective-permute-start | bytes 1179656 | tf_op jit(solution)/shard_map/ppermute | solution.py:376
  76.9 16.8 %collective-permute-start.5 = (bf16[96,2048]{1,0:T(8,128)(2,1)S(1)}, bf16[96,2048]{1,0:T(8,128)(2,1)S(1)}, u32[]{:S(2)}, u32[]{:S(2)}) collective-permute-start(bf16[96,2048]{1,0:T(8,128)(2,1)S(1)} %get-tuple-element.33), channel_id=1, source_target_pairs={{0,14},{1,15},{2,0},{3,1},{4,2},{5,3},{6,4},{7,5},{8,6},{9,7},{10,... | collective-permute-start | bytes 1179656 | tf_op jit(solution)/shard_map/ppermute | solution.py:377
  81.8 21.3 %collective-permute-start.18 = (bf16[160,2048]{1,0:T(8,128)(2,1)S(1)}, bf16[160,2048]{1,0:T(8,128)(2,1)S(1)}, u32[]{:S(2)}, u32[]{:S(2)}) collective-permute-start(bf16[160,2048]{1,0:T(8,128)(2,1)S(1)} %get-tuple-element.41), channel_id=1, source_target_pairs={{0,1},{1,0},{2,3},{3,2},{4,5},{5,4},{6,7},{7,6},{8,9},{9,8},{10,11... | collective-permute-start | bytes 1966088 | tf_op jit(solution)/shard_map/ppermute | solution.py:386
  85.2 11.2 %collective-permute-start.16 = (bf16[32,2048]{1,0:T(8,128)(2,1)S(1)}, bf16[32,2048]{1,0:T(8,128)(2,1)S(1)}, u32[]{:S(2)}, u32[]{:S(2)}) collective-permute-start(bf16[32,2048]{1,0:T(8,128)(2,1)S(1)} %slice.90), channel_id=1, source_target_pairs={{0,2},{1,3},{2,4},{3,5},{4,6},{5,7},{6,8},{7,9},{8,10},{9,11},{10,... | collective-permute-start | bytes 393224 | tf_op jit(solution)/shard_map/ppermute | solution.py:378
  85.3 21.3 %collective-permute-start.8 = (bf16[160,2048]{1,0:T(8,128)(2,1)S(1)}, bf16[160,2048]{1,0:T(8,128)(2,1)S(1)}, u32[]{:S(2)}, u32[]{:S(2)}) collective-permute-start(bf16[160,2048]{1,0:T(8,128)(2,1)S(1)} %get-tuple-element.35), channel_id=1, source_target_pairs={{0,1},{1,0},{2,3},{3,2},{4,5},{5,4},{6,7},{7,6},{8,9},{9,8},{10,11... | collective-permute-start | bytes 1966088 | tf_op jit(solution)/shard_map/ppermute | solution.py:386
  93.7 7.3 %collective-permute-start.6 = (bf16[32,2048]{1,0:T(8,128)(2,1)S(1)}, bf16[32,2048]{1,0:T(8,128)(2,1)S(1)}, u32[]{:S(2)}, u32[]{:S(2)}) collective-permute-start(bf16[32,2048]{1,0:T(8,128)(2,1)S(1)} %slice.88), channel_id=1, source_target_pairs={{0,2},{1,3},{2,4},{3,5},{4,6},{5,7},{6,8},{7,9},{8,10},{9,11},{10,... | collective-permute-start | bytes 393224 | tf_op jit(solution)/shard_map/ppermute | solution.py:378
  96.5 5.2 %collective-permute-start.7 = (bf16[32,2048]{1,0:T(8,128)(2,1)S(1)}, bf16[32,2048]{1,0:T(8,128)(2,1)S(1)}, u32[]{:S(2)}, u32[]{:S(2)}) collective-permute-start(bf16[32,2048]{1,0:T(8,128)(2,1)S(1)} %slice.89), channel_id=1, source_target_pairs={{0,14},{1,15},{2,0},{3,1},{4,2},{5,3},{6,4},{7,5},{8,6},{9,7},{10,... | collective-permute-start | bytes 393224 | tf_op jit(solution)/shard_map/ppermute | solution.py:379
  97.5 5.6 %collective-permute-start.19 = (bf16[96,2048]{1,0:T(8,128)(2,1)S(1)}, bf16[96,2048]{1,0:T(8,128)(2,1)S(1)}, u32[]{:S(2)}, u32[]{:S(2)}) collective-permute-start(bf16[96,2048]{1,0:T(8,128)(2,1)S(1)} %get-tuple-element.42), channel_id=1, source_target_pairs={{0,1},{1,0},{2,3},{3,2},{4,5},{5,4},{6,7},{7,6},{8,9},{9,8},{10,11... | collective-permute-start | bytes 1179656 | tf_op jit(solution)/shard_map/ppermute | solution.py:393
  101.7 4.9 %collective-permute-start.9 = (bf16[96,2048]{1,0:T(8,128)(2,1)S(1)}, bf16[96,2048]{1,0:T(8,128)(2,1)S(1)}, u32[]{:S(2)}, u32[]{:S(2)}) collective-permute-start(bf16[96,2048]{1,0:T(8,128)(2,1)S(1)} %get-tuple-element.36), channel_id=1, source_target_pairs={{0,1},{1,0},{2,3},{3,2},{4,5},{5,4},{6,7},{7,6},{8,9},{9,8},{10,11... | collective-permute-start | bytes 1179656 | tf_op jit(solution)/shard_map/ppermute | solution.py:393
  121.8 54.6 %all-to-all-start = ((bf16[16,32,2048]{2,1,0:T(8,128)(2,1)}), bf16[16,32,2048]{2,1,0:T(8,128)(2,1)S(1)}, u32[]{:S(2)}, u32[]{:S(2)}) async-start(bf16[16,32,2048]{2,1,0:T(8,128)(2,1)} %copy-done.5), calls=%async_computation | async-start | bytes 4194304 | tf_op jit(solution)/shard_map/all_to_all | solution.py:440
  178.5 17.2 %all-to-all-start.1 = ((bf16[16,128,128]{2,1,0:T(8,128)(2,1)}), bf16[16,128,128]{2,1,0:T(8,128)(2,1)S(1)}, u32[]{:S(2)}, u32[]{:S(2)}) async-start(bf16[16,128,128]{2,1,0:T(8,128)(2,1)} %undo.1), calls=%async_computation.1 | async-start | bytes 1048576 | tf_op jit(solution)/shard_map/all_to_all | solution.py:464
  196.7 16.4 %all-to-all-start.2 = ((bf16[16,128,128]{2,1,0:T(8,128)(2,1)}), bf16[16,128,128]{2,1,0:T(8,128)(2,1)S(1)}, u32[]{:S(2)}, u32[]{:S(2)}) async-start(bf16[16,128,128]{2,1,0:T(8,128)(2,1)} %temporal.1), calls=%async_computation.2 | async-start | bytes 1048576 | tf_op jit(solution)/shard_map/all_to_all | solution.py:468
  220.1 17.6 %all-to-all-start.3 = ((f32[16,16,128]{2,1,0:T(8,128)}), f32[16,16,128]{2,1,0:T(8,128)S(1)}, u32[]{:S(2)}, u32[]{:S(2)}) async-start(f32[16,16,128]{2,1,0:T(8,128)} %get-tuple-element.49), calls=%async_computation.3 | async-start | bytes 262144 | tf_op jit(solution)/shard_map/all_to_all | solution.py:475
  (30 other events, 263.8 us)
Sparse Core Ops, SparseCore 0:
  121.8 93.2 reduce-scatter.1
